TPU v7x, 512 devices: a whole 4x8x8 slice. The times are simulated.
512 devices in a mesh: ab: 16 (over z, x_hi), ij: 16 (over y, core), rep: 2 (over x_lo).
Axes of the slice: x: 4 (x_hi: 2, x_lo: 2; x = x_hi * 2 + x_lo), y: 8, z: 8, core: 2. Of those that a mesh axis runs over, the one named last changes fastest.
Arguments:
- cholesky_a: bfloat16 [512, 64, 4096], P(('rep', 'ab'), None, 'ij'), parts along dimension 0, may hold values from -0.75 to 0.75
- cholesky_b: bfloat16 [24, 64, 4096], P('rep', None, 'ij'), parts along dimension 0, may hold values from -0.75 to 0.75
- amplitudes: bfloat16 [64, 64, 4096], P('ab', None, 'ij'), may hold values from -0.09375 to 0.09375
- other_terms: float32 [512, 12, 4096], P(('rep', 'ab'), None, 'ij'), parts along dimension 0, may hold values from -6 to 6
- virtual_a: float32 [512], P(('rep', 'ab')), parts along dimension 0, may hold values from 0.2 to 2
- virtual_b: float32 [24], P('rep'), parts along dimension 0, may hold values from 0.2 to 2
- pair_energy: float32 [4096], P('ij'), may hold values from -1.5 to -0.2
Outputs:
- residual: float32 [512, 12, 4096], P(('rep', 'ab'), None, 'ij'), parts along dimension 0
- update: float32 [512, 12, 4096], P(('rep', 'ab'), None, 'ij'), parts along dimension 0
There are 2 independent parts, one for each index of `rep`. A program takes and returns all parts, laid end to end along the dimension named above; an argument that names none is the same for every part. Nothing has to cross between parts.
All inputs are finite; a program needn't handle non-finite values.
Results may differ from a plain program's by a relative error of at most 0.014.
Values may be sent and summed in bfloat16 or wider, within the bound.
A program may use at most 64 MiB of HBM per device.

v0:
```python
import jax
import jax.numpy as jnp
from jax import lax
from jax.sharding import PartitionSpec as P


def shards(cholesky_a, cholesky_b, amplitudes, other_terms, virtual_a, virtual_b, pair_energy):
    a_rows, c_count, _ = cholesky_a.shape
    b_rows, d_count, _ = cholesky_b.shape
    left = lax.all_gather(cholesky_a, "ij", axis=2, tiled=True)
    right = lax.all_gather(cholesky_b, "ij", axis=2, tiled=True)
    summed = lax.dot_general(
        left.reshape(a_rows * c_count, left.shape[2]),
        right.reshape(b_rows * d_count, right.shape[2]),
        (((1,), (1,)), ((), ())),
        preferred_element_type=jnp.float32,
    )
    integrals = summed.astype(jnp.bfloat16).reshape(a_rows, c_count, b_rows, d_count)
    ladder = jnp.einsum(
        "acbd,cdj->abj",
        integrals,
        lax.all_gather(amplitudes, "ab", axis=0, tiled=True),
        preferred_element_type=jnp.float32,
    )
    residual = other_terms + ladder
    divisor = virtual_a[:, None, None] + virtual_b[None, :, None] - pair_energy[None, None, :]
    return (residual, residual / divisor)


def solution(mesh):
    return jax.shard_map(
        shards,
        mesh=mesh,
        in_specs=(
            P(("rep", "ab"), None, "ij"),
            P("rep", None, "ij"),
            P("ab", None, "ij"),
            P(("rep", "ab"), None, "ij"),
            P(("rep", "ab")),
            P("rep"),
            P("ij"),
        ),
        out_specs=(P(("rep", "ab"), None, "ij"), P(("rep", "ab"), None, "ij")),
        check_vma=False,
    )
```

profile of v0, /device:TPU:1, one launch (start us, length us, event | category | flops | bytes accessed | tf_op | source)
XLA Modules:
  0.0 244.2 jit_solution(15328190173590800572)
XLA Ops:
  7.2 0.0 all-gather.6.cloned.1.call-start
  7.2 0.7 all-gather.6.cloned.1.call-update
  7.9 0.0 all-gather.4.cloned.1.call-start
  7.9 0.7 all-gather.4.cloned.1.call-update
  8.6 0.0 all-gather.8.cloned.1.call-start
  8.7 0.7 all-gather.8.cloned.1.call-update
  9.4 0.7 broadcast_add_fusion
  10.1 64.8 %all-gather.6.cloned.1.call-done = bf16[12,64,4096]{2,1,0:T(8,128)(2,1)} async-done(((bf16[12,64,256]{2,1,0:T(8,128)(2,1)}), bf16[12,64,4096]{2,1,0:T(8,128)(2,1)}) %all-gather.6.cloned.1.call-update) | async-done | bytes 6291472 | tf_op jit(solution)/shard_map/all_gather | solution.py:11
  74.9 69.2 %all-gather.4.cloned.1.call-done = bf16[16,64,4096]{2,1,0:T(8,128)(2,1)} async-done(((bf16[16,64,256]{2,1,0:T(8,128)(2,1)}), bf16[16,64,4096]{2,1,0:T(8,128)(2,1)}) %all-gather.4.cloned.1.call-update) | async-done | bytes 8388624 | tf_op jit(solution)/shard_map/all_gather | solution.py:10
  144.1 11.0 %convolution_convert_fusion = bf16[1024,768]{1,0:T(8,128)(2,1)S(1)} fusion(bf16[1024,4096]{1,0:T(8,128)(2,1)} %bitcast.21, bf16[768,4096]{1,0:T(8,128)(2,1)} %bitcast.22), kind=kOutput, calls=%fused_computation.3 | convolution fusion | flops 6443237376 | bytes 16252928 | tf_op jit(solution)/shard_map/dot_general | solution.py:12
  155.1 0.8 copy.12
  155.9 0.0 copy-start
  155.9 0.0 copy-start.1
  155.9 3.3 %reshape.48 = bf16[16,64,12,64]{1,0,3,2:T(8,128)(2,1)} reshape(bf16[1024,768]{0,1:T(8,128)(2,1)S(1)} %copy.12) | data formatting | bytes 3145728 | tf_op jit(solution)/shard_map/reshape | solution.py:18
  159.2 72.5 %all-gather.8.cloned.1.call-done = bf16[64,64,256]{2,1,0:T(8,128)(2,1)} async-done(((bf16[4,64,256]{2,1,0:T(8,128)(2,1)}), bf16[64,64,256]{2,1,0:T(8,128)(2,1)}) %all-gather.8.cloned.1.call-update) | async-done | bytes 2097168 | tf_op jit(solution)/shard_map/all_gather | solution.py:22
  231.8 0.0 copy-done
  231.8 0.0 copy-done.1
  231.8 5.9 %subtract_divide_fusion = (f32[16,12,256]{2,0,1:T(8,128)}, f32[16,12,256]{2,0,1:T(8,128)}) fusion(f32[256]{0:T(256)S(1)} %copy-done.1, f32[16,12]{0,1:T(8,128)S(1)} %broadcast_add_fusion, f32[16,12,256]{2,0,1:T(8,128)S(1)} %copy-done, bf16[16,64,12,64]{1,0,3,2:T(8,128)(2,1)} %reshape.48, bf16[64,64,256]{2,1,0:T(8,128)(2,1)} %all-gather.8.cloned.1.call-done), kind=kOutput, calls=%fused_computation.6 | convolution fusion | flops 402800640 | bytes 4261632 | tf_op jit(solution)/shard_map/acbd,cdj->abj/dot_general | solution.py:19
Async XLA Ops:
  7.2 67.7 %all-gather.6.cloned.1.call-start = ((), (), s32[]{:S(2)}) async-start(), calls=%async_computation.1 | async-start | bytes 6684672 | tf_op jit(solution)/shard_map/all_gather | solution.py:11
  7.9 136.2 %all-gather.4.cloned.1.call-start = ((), (), s32[]{:S(2)}) async-start(), calls=%async_computation | async-start | bytes 8912896 | tf_op jit(solution)/shard_map/all_gather | solution.py:10
  8.6 223.1 %all-gather.8.cloned.1.call-start = ((), (), s32[]{:S(2)}) async-start(), calls=%async_computation.2 | async-start | bytes 2228224 | tf_op jit(solution)/shard_map/all_gather | solution.py:22
  155.9 75.9 %copy-start = (f32[16,12,256]{2,0,1:T(8,128)S(1)}, f32[16,12,256]{2,0,1:T(8,128)}, u32[]{:S(2)}) copy-start(f32[16,12,256]{2,0,1:T(8,128)} %param.10) | copy-start | bytes 589828
  155.9 75.9 %copy-start.1 = (f32[256]{0:T(256)S(1)}, f32[256]{0:T(256)}, u32[]{:S(2)}) copy-start(f32[256]{0:T(256)} %param.13) | copy-start | bytes 3076
Sparse Core Ops, SparseCore 0:
  10.0 64.8 all-gather.5
  77.0 67.1 all-gather.3
  147.3 84.4 all-gather.7
where the time goes:
time: 247 us; the launch traced here: 244 us
  waiting for transfers between devices  209 us (85%)
  matrix products  16.9 us (7%)
  between operations  13.8 us (6%)
  local copies, waits for them, and re-layouts  4.07 us (2%)
    all_gather x1, waiting for transfers between devices, shards(): lax.all_gather(amplitudes, 'ab', axis=0, tiled=True)  72.5 us
    all_gather x1, waiting for transfers between devices, shards(): left = lax.all_gather(cholesky_a, 'ij', axis=2, tiled=True)  69.2 us
    all_gather x1, waiting for transfers between devices, shards(): right = lax.all_gather(cholesky_b, 'ij', axis=2, tiled=True)  64.8 us
    dot_general x1, matrix products, shards(): lax.dot_general(left.reshape(a_rows * c_count, left.shape[2]), right.resh...  11 us
    dot_general x1, matrix products, shards(): jnp.einsum('acbd,cdj->abj', integrals, lax.all_gather(amplitudes, 'ab', a...  5.91 us
  transfers between devices with their start and end apart: 3, of which 3 were waited for; matrix products, arithmetic and copies ran while one was open for 6% of the time, Pallas kernels for 0%

commit v1 on v0

v1 whole, which is shorter than its diff:
```python
import functools

import jax
import jax.numpy as jnp
from jax import lax
from jax.experimental import pallas as pl
from jax.experimental.pallas import tpu as pltpu
from jax.sharding import PartitionSpec as P

MESH = pl.DeviceIdType.MESH
BF16, F32 = jnp.bfloat16, jnp.float32
RING = 8
LONG = {1: 0, -1: 1}


def dot(a, b, dims):
    return lax.dot_general(a, b, (dims, ((), ())), preferred_element_type=F32)


def kernel(n_msg, a_hbm, b_hbm, t_hbm, out_ref,
           a_own, a_sib, b_own, b_sib, a_perm, part, rs_in, rs_out, gath, t_all, acc,
           send_sem, recv_sem, load_sem):
    ab, ij, lo = lax.axis_index("ab"), lax.axis_index("ij"), lax.axis_index("rep")
    z, hi = ab // 2, ab % 2
    y, core = ij // 2, ij % 2
    sibling = (ab, y * 2 + 1 - core, lo)
    y_next = {s: (ab, ((y + s + RING) % RING) * 2 + core, lo) for s in (1, -1)}
    z_next = {s: (((z + s + RING) % RING) * 2 + hi, ij, lo) for s in (1, -1)}
    x_far = (z * 2 + 1 - hi, ij, 1 - lo)
    x_near = (ab, ij, 1 - lo)

    started, ids = [], {}

    def send(name, src, dst, device):
        number = ids.setdefault(name, len(ids))
        copy = pltpu.make_async_remote_copy(
            src_ref=src, dst_ref=dst, send_sem=send_sem.at[number], recv_sem=recv_sem.at[number],
            device_id=device, device_id_type=MESH,
        )
        copy.start()
        started.append(copy)
        arrivals[name] = copy

    arrivals = {}

    def arrived(name):
        arrivals[name].wait_recv()

    half_a = pl.ds(pl.multiple_of(core * 32, 32), 32)
    other_half_a = pl.ds(pl.multiple_of(32 - core * 32, 32), 32)
    load_a = pltpu.make_async_copy(a_hbm.at[:, half_a], a_own, load_sem.at[0])
    load_b = pltpu.make_async_copy(b_hbm, b_own, load_sem.at[1])
    load_t = pltpu.make_async_copy(t_hbm, t_all.at[ab], load_sem.at[2])
    load_a.start()
    load_b.start()
    load_t.start()

    barrier = pltpu.get_barrier_semaphore()
    friends = (sibling, y_next[1], y_next[-1], z_next[1], z_next[-1], x_far, x_near)
    for friend in friends:
        pl.semaphore_signal(barrier, inc=1, device_id=friend, device_id_type=MESH)
    pl.semaphore_wait(barrier, len(friends))

    send("a", a_hbm.at[:, other_half_a], a_sib, sibling)
    send("b", b_hbm, b_sib, sibling)

    def t_rows(half):
        return pl.ds(half * 128, 128)

    t_far = pl.ds(pl.multiple_of((1 - lo) * 128, 128), 128)
    t_near = pl.ds(pl.multiple_of(lo * 128, 128), 128)

    def t_send_z(s, stage, half):
        slab = ((z - s * stage + 2 * RING) % RING) * 2 + hi
        src = t_hbm.at[t_rows(half)] if stage == 0 else t_all.at[slab, t_rows(half)]
        send(("z", s, stage, half), src, t_all.at[slab, t_rows(half)], z_next[s])

    def t_send_far(offset):
        slab = ((z + offset + RING) % RING) * 2 + hi
        src = t_hbm.at[t_far] if offset == 0 else t_all.at[slab, t_far]
        send(("far", offset), src, t_all.at[slab, t_far], x_far)

    def t_send_near(offset):
        arrived(("far", offset))
        slab = ((z + offset + RING) % RING) * 2 + 1 - hi
        send(("near", offset), t_all.at[slab, t_near], t_all.at[slab, t_near], x_near)

    def t_stage(stage):
        for s in (1, -1):
            arrived(("z", s, stage, LONG[s]))
            if stage < 3:
                t_send_z(s, stage + 1, LONG[s])
        if stage < 3:
            for s in (1, -1):
                arrived(("z", s, stage, 1 - LONG[s]))
                if stage < 2:
                    t_send_z(s, stage + 1, 1 - LONG[s])
                t_send_far(-s * (stage + 1))
        else:
            t_send_far(4)

    for s in (1, -1):
        t_send_z(s, 0, LONG[s])
    t_send_far(0)
    for s in (1, -1):
        t_send_z(s, 0, 1 - LONG[s])

    row = lax.broadcasted_iota(jnp.int32, (256, 256), 0)
    column = lax.broadcasted_iota(jnp.int32, (256, 256), 1)
    swap = jnp.where(column == (row % 16) * 16 + row // 16, 1.0, 0.0).astype(BF16)

    def reorder(ref, place):
        for block in range(2):
            rows = ref[:, block * 16:(block + 1) * 16, :].reshape(256, 256)
            a_perm[place, block * 256:(block + 1) * 256, :] = dot(swap, rows, ((1,), (0,))).astype(BF16)

    load_a.wait()
    reorder(a_own, 0)
    load_b.wait()
    part[...] = dot(a_perm[0], b_own[...], ((1,), (1,)))
    arrived("a")
    reorder(a_sib, 1)
    arrived("b")
    part[...] += dot(a_perm[1], b_sib[...], ((1,), (1,)))

    def rs_slot(s, stage, half):
        long = half == LONG[s]
        return (0 if s == 1 else 7) + (stage if long else 4 + stage)

    def rs_send(s, stage, half):
        distance = (4 if half == LONG[s] else 3) - stage
        owner = (y + s * distance + RING) % RING
        rows = pl.ds(pl.multiple_of(owner * 64 + half * 32, 32), 32)
        value = part[rows, :]
        if stage:
            arrived(("rs", s, stage - 1, half))
            value = value + rs_in[rs_slot(s, stage - 1, half)].astype(F32)
        slot = rs_slot(s, stage, half)
        rs_out[slot] = value.astype(BF16)
        send(("rs", s, stage, half), rs_out.at[slot], rs_in.at[slot], y_next[s])

    def rs_stage(stage):
        for s in (1, -1):
            rs_send(s, stage, LONG[s])
        if stage < 3:
            for s in (1, -1):
                rs_send(s, stage, 1 - LONG[s])

    rs_stage(0)
    t_stage(0)
    rs_stage(1)
    t_send_near(0)
    t_stage(1)
    rs_stage(2)
    for offset in (-1, 1):
        t_send_near(offset)
    t_stage(2)
    rs_stage(3)

    me = core * RING + y
    total = []
    for half in range(2):
        value = part[pl.ds(pl.multiple_of(y * 64 + half * 32, 32), 32), :]
        for s in (1, -1):
            last = 3 if half == LONG[s] else 2
            arrived(("rs", s, last, half))
            value = value + rs_in[rs_slot(s, last, half)].astype(F32)
        total.append(value)
    total = jnp.concatenate(total, axis=0)
    for b in range(12):
        block = jnp.concatenate([total[c * 16:(c + 1) * 16, b * 64:(b + 1) * 64] for c in range(4)], axis=1)
        gath[me, b * 16:(b + 1) * 16, :] = block.astype(BF16)

    def g_rows(half):
        return pl.ds(half * 96, 96)

    def g_send(s, stage, half):
        slab = core * RING + (y - s * stage + RING) % RING
        ref = gath.at[slab, g_rows(half)]
        send(("g", s, stage, half), ref, ref, y_next[s])

    def g_sib(offset):
        slab = core * RING + (y + offset + RING) % RING
        send(("gs", offset), gath.at[slab], gath.at[slab], sibling)

    def ladder(offset, other):
        slab = (1 - core if other else core) * RING + (y + offset + RING) % RING
        return dot(gath[slab], t_all[slab], ((1,), (0,)))

    for s in (1, -1):
        g_send(s, 0, LONG[s])
    for s in (1, -1):
        g_send(s, 0, 1 - LONG[s])
    g_sib(0)

    for offset in (-2, 2):
        t_send_near(offset)
    t_stage(3)
    for offset in (-3, 3, 4):
        t_send_near(offset)

    for stage in range(4):
        for s in (1, -1):
            arrived(("g", s, stage, LONG[s]))
            if stage < 3:
                g_send(s, stage + 1, LONG[s])
        if stage < 3:
            for s in (1, -1):
                arrived(("g", s, stage, 1 - LONG[s]))
                if stage < 2:
                    g_send(s, stage + 1, 1 - LONG[s])
                g_sib(-s * (stage + 1))
        else:
            g_sib(4)
        if stage == 0:
            load_t.wait()
            for offset in (0, -1, 1, -2, 2, -3, 3, 4):
                arrived(("near", offset))
            acc[...] = ladder(0, False)
        if stage < 3:
            acc[...] += ladder(-stage - 1, False) + ladder(stage + 1, False)
        else:
            acc[...] += ladder(4, False)
        for offset in ((0,), (-1, 1), (-2, 2), (-3, 3))[stage]:
            arrived(("gs", offset))
            acc[...] += ladder(offset, True)
    arrived(("gs", 4))
    out_ref[...] = acc[...] + ladder(4, True)

    for copy in started:
        copy.wait_send()
    assert len(ids) == n_msg


def shards(cholesky_a, cholesky_b, amplitudes, other_terms, virtual_a, virtual_b, pair_energy):
    n_msg = 2 + 14 + 8 + 8 + 14 + 14 + 8
    any_spec = pl.BlockSpec(memory_space=pl.ANY)
    ladder = pl.pallas_call(
        functools.partial(kernel, n_msg),
        out_shape=jax.ShapeDtypeStruct((192, 256), F32),
        in_specs=[any_spec] * 3,
        out_specs=pl.BlockSpec(memory_space=pltpu.VMEM),
        scratch_shapes=[
            pltpu.VMEM((16, 32, 256), BF16),
            pltpu.VMEM((16, 32, 256), BF16),
            pltpu.VMEM((768, 256), BF16),
            pltpu.VMEM((768, 256), BF16),
            pltpu.VMEM((2, 512, 256), BF16),
            pltpu.VMEM((512, 768), F32),
            pltpu.VMEM((14, 32, 768), BF16),
            pltpu.VMEM((14, 32, 768), BF16),
            pltpu.VMEM((16, 192, 256), BF16),
            pltpu.VMEM((16, 256, 256), BF16),
            pltpu.VMEM((192, 256), F32),
            pltpu.SemaphoreType.DMA((n_msg,)),
            pltpu.SemaphoreType.DMA((n_msg,)),
            pltpu.SemaphoreType.DMA((3,)),
        ],
        compiler_params=pltpu.CompilerParams(
            collective_id=0, has_side_effects=True, vmem_limit_bytes=40 * 2**20
        ),
        cost_estimate=pl.CostEstimate(flops=2 * 512 * 512 * 768 + 2 * 192 * 4096 * 256, bytes_accessed=2**21, transcendentals=0),
    )(cholesky_a, cholesky_b.reshape(768, 256), amplitudes.reshape(256, 256))
    ladder = ladder.reshape(12, 16, 256).transpose(1, 0, 2)
    residual = other_terms + ladder
    divisor = virtual_a[:, None, None] + virtual_b[None, :, None] - pair_energy[None, None, :]
    return (residual, residual / divisor)


def solution(mesh):
    return jax.shard_map(
        shards,
        mesh=mesh,
        in_specs=(
            P(("rep", "ab"), None, "ij"),
            P("rep", None, "ij"),
            P("ab", None, "ij"),
            P(("rep", "ab"), None, "ij"),
            P(("rep", "ab")),
            P("rep"),
            P("ij"),
        ),
        out_specs=(P(("rep", "ab"), None, "ij"), P(("rep", "ab"), None, "ij")),
        check_vma=False,
    )
```

time: 247 us -> 54.5 us (0.22); the launches traced: 244 us -> 54.2 us
  waiting for transfers between devices: 209 us -> 0 us
  Pallas kernels: 0 us -> 48.4 us
  matrix products: 16.9 us -> 0 us
  between operations: 13.8 us -> 0.68 us
    all_gather x3 -> x0, waiting for transfers between devices: 207 us -> none  [the longest x1 72.5 us: shards(): lax.all_gather(amplitudes, 'ab', axis=0, tiled=True)]
    pallas_call x0 -> x1, Pallas kernels: none -> 48.4 us  [shards(): pl.pallas_call(functools.partial(kernel, n_msg), out_shape=jax.ShapeDtype...]
    dot_general x2 -> x0, matrix products: 16.9 us -> none  [the longest x1 11 us: shards(): lax.dot_general(left.reshape(a_rows * c_count, left.shape[2]), right.resh...]
    unnamed x4 -> x14, local copies, waits for them, and re-layouts: 0.01 us -> 4.27 us
    reshape x1 -> x0, local copies, waits for them, and re-layouts: 3.3 us -> none  [shards(): summed.astype(jnp.bfloat16).reshape(a_rows, c_count, b_rows, d_count)]
  transfers between devices with their start and end apart: 3 -> 0, of which waited for: 3 -> 0; matrix products, arithmetic and copies ran while one was open for 6% -> 0% of each run, Pallas kernels for 0% -> 0%
where the time goes in v1:
time: 54.5 us; the launch traced here: 54.2 us
  Pallas kernels  48.4 us (89%)
  local copies, waits for them, and re-layouts  4.27 us (8%)
  other arithmetic  0.85 us (2%)
  between operations  0.68 us (1%)
    pallas_call x1, Pallas kernels, shards(): pl.pallas_call(functools.partial(kernel, n_msg), out_shape=jax.ShapeDtype...  48.4 us
    unnamed x14, local copies, waits for them, and re-layouts  4.27 us

profile of v1, /device:TPU:1, one launch (start us, length us, event | category | flops | bytes accessed | tf_op | source)
XLA Modules:
  0.0 54.2 jit_solution(268721126235747370)
XLA Ops:
  0.6 0.0 copy-start.5
  0.6 0.0 copy-start.6
  0.6 0.6 %copy-done.5 = f32[12]{0:T(128)S(1)} copy-done((f32[12]{0:T(128)S(1)}, f32[12]{0:T(128)}, u32[]{:S(2)}) %copy-start.5) | copy-done | bytes 72
  1.3 0.0 copy-done.6
  1.3 0.1 broadcast_add_fusion
  1.4 0.0 copy-start
  1.4 1.0 %copy-done = bf16[16,64,256]{2,1,0:T(8,128)(2,1)S(1)} copy-done((bf16[16,64,256]{2,1,0:T(8,128)(2,1)S(1)}, bf16[16,64,256]{2,1,0:T(8,128)(2,1)}, u32[]{:S(2)}) %copy-start) | copy-done | bytes 524312
  2.4 0.0 copy-start.1
  2.4 1.0 %copy-done.1 = bf16[12,64,256]{2,1,0:T(8,128)(2,1)S(1)} copy-done((bf16[12,64,256]{2,1,0:T(8,128)(2,1)S(1)}, bf16[12,64,256]{2,1,0:T(8,128)(2,1)}, u32[]{:S(2)}) %copy-start.1) | copy-done | bytes 393240
  3.4 0.0 copy-start.2
  3.4 0.9 %copy-done.2 = bf16[4,64,256]{2,1,0:T(8,128)(2,1)S(1)} copy-done((bf16[4,64,256]{2,1,0:T(8,128)(2,1)S(1)}, bf16[4,64,256]{2,1,0:T(8,128)(2,1)}, u32[]{:S(2)}) %copy-start.2) | copy-done | bytes 131096
  4.3 0.0 copy-start.3
  4.3 48.4 %shard_map.86 = f32[192,256]{1,0:T(8,128)S(1)} custom-call(bf16[16,64,256]{2,1,0:T(8,128)(2,1)S(1)} %copy-done, bf16[768,256]{1,0:T(8,128)(2,1)S(1)} %bitcast.6, bf16[256,256]{1,0:T(8,128)(2,1)S(1)} %bitcast.7), custom_call_target="tpu_custom_call" | custom-call | flops 805306368 | bytes 2097152 | tf_op jit(solution)/shard_map/pallas_call | solution.py:238
  52.8 0.0 copy-start.4
  52.8 0.0 copy-done.3
  52.8 0.7 %copy-done.4 = f32[256]{0:T(256)S(1)} copy-done((f32[256]{0:T(256)S(1)}, f32[256]{0:T(256)}, u32[]{:S(2)}) %copy-start.4) | copy-done | bytes 1048
  53.4 0.8 %subtract_divide_fusion = (f32[16,12,256]{2,0,1:T(8,128)}, f32[16,12,256]{2,0,1:T(8,128)}) fusion(f32[256]{0:T(256)S(1)} %copy-done.4, f32[16,12]{0,1:T(8,128)S(1)} %broadcast_add_fusion, f32[16,12,256]{2,0,1:T(8,128)S(1)} %copy-done.3, f32[16,12,256]{2,0,1:T(8,128)S(1)} %bitcast.5), kind=kLoop, calls=%fused_computation | loop fusion | flops 147456 | bytes 788224 | tf_op jit(solution)/shard_map/div | solution.py:267
Async XLA Ops:
  0.6 0.7 %copy-start.5 = (f32[12]{0:T(128)S(1)}, f32[12]{0:T(128)}, u32[]{:S(2)}) copy-start(f32[12]{0:T(128)} %param.12) | copy-start | bytes 148
  0.6 0.7 %copy-start.6 = (f32[16]{0:T(128)S(1)}, f32[16]{0:T(128)}, u32[]{:S(2)}) copy-start(f32[16]{0:T(128)} %param.11) | copy-start | bytes 196
  1.4 1.0 %copy-start = (bf16[16,64,256]{2,1,0:T(8,128)(2,1)S(1)}, bf16[16,64,256]{2,1,0:T(8,128)(2,1)}, u32[]{:S(2)}) copy-start(bf16[16,64,256]{2,1,0:T(8,128)(2,1)} %a_hbm.1) | copy-start | bytes 1572868
  2.4 1.0 %copy-start.1 = (bf16[12,64,256]{2,1,0:T(8,128)(2,1)S(1)}, bf16[12,64,256]{2,1,0:T(8,128)(2,1)}, u32[]{:S(2)}) copy-start(bf16[12,64,256]{2,1,0:T(8,128)(2,1)} %param.8) | copy-start | bytes 1179652
  3.4 0.9 %copy-start.2 = (bf16[4,64,256]{2,1,0:T(8,128)(2,1)S(1)}, bf16[4,64,256]{2,1,0:T(8,128)(2,1)}, u32[]{:S(2)}) copy-start(bf16[4,64,256]{2,1,0:T(8,128)(2,1)} %param.9) | copy-start | bytes 393220
  4.3 48.5 %copy-start.3 = (f32[16,12,256]{2,0,1:T(8,128)S(1)}, f32[16,12,256]{2,0,1:T(8,128)}, u32[]{:S(2)}) copy-start(f32[16,12,256]{2,0,1:T(8,128)} %param.10) | copy-start | bytes 589828
  52.8 0.7 %copy-start.4 = (f32[256]{0:T(256)S(1)}, f32[256]{0:T(256)}, u32[]{:S(2)}) copy-start(f32[256]{0:T(256)} %param.13) | copy-start | bytes 3076

commit v2 on v0

v2 whole, which is shorter than its diff:
```python
import jax
import jax.numpy as jnp
from jax import lax
from jax.experimental import pallas as pl
from jax.experimental.pallas import tpu as pltpu
from jax.sharding import PartitionSpec as P

MESH = pl.DeviceIdType.MESH
BF16, F32 = jnp.bfloat16, jnp.float32
RING = 8
PIECES = 4
LONG = {1: (0, 1), -1: (2, 3)}
SHORT = {1: (2, 3), -1: (0, 1)}
T_LONG = {1: 0, -1: 1}
N_RECV, N_SEND = 68, 8


def dot(a, b, dims):
    return lax.dot_general(a, b, (dims, ((), ())), preferred_element_type=F32)


def rotation(pieces):
    return [(s, pieces[s][i]) for i in range(PIECES // 2) for s in (1, -1)]


def kernel(a_hbm, b_hbm, t_hbm, va_hbm, vb_hbm, pe_hbm, out_ref, div_ref,
           va_ref, vb_ref, pe_ref, a_in, a_all, b_all, part, rs_in, rs_out, gath, t_all,
           send_sem, recv_sem, load_sem):
    ab, ij, lo = lax.axis_index("ab"), lax.axis_index("ij"), lax.axis_index("rep")
    z, hi = ab // 2, ab % 2
    y, core = ij // 2, ij % 2
    sibling = (ab, y * 2 + 1 - core, lo)
    y_next = {s: (ab, ((y + s + RING) % RING) * 2 + core, lo) for s in (1, -1)}
    z_next = {s: (((z + s + RING) % RING) * 2 + hi, ij, lo) for s in (1, -1)}
    x_far = (z * 2 + 1 - hi, ij, 1 - lo)
    x_near = (ab, ij, 1 - lo)
    x_near_sibling = (ab, y * 2 + 1 - core, 1 - lo)

    numbers = ({}, {})

    def recv_of(to, name):
        return recv_sem.at[numbers[to].setdefault(name, len(numbers[to]))]

    def send(to, name, src, dst, device, group):
        pltpu.make_async_remote_copy(
            src_ref=src, dst_ref=dst, send_sem=send_sem.at[group], recv_sem=recv_of(to, name),
            device_id=device, device_id_type=MESH,
        ).start()

    def arrived(to, name, ref):
        pltpu.make_async_remote_copy(
            src_ref=ref, dst_ref=ref, send_sem=send_sem.at[0], recv_sem=recv_of(to, name),
            device_id=sibling, device_id_type=MESH,
        ).wait_recv()

    def sent(group, ref):
        pltpu.make_async_remote_copy(
            src_ref=ref, dst_ref=ref, send_sem=send_sem.at[group], recv_sem=recv_sem.at[0],
            device_id=sibling, device_id_type=MESH,
        ).wait_send()

    def meet(friends):
        barrier = pltpu.get_barrier_semaphore()
        for friend in friends:
            pl.semaphore_signal(barrier, inc=1, device_id=friend, device_id_type=MESH)
        pl.semaphore_wait(barrier, len(friends))

    load_a = pltpu.make_async_copy(a_hbm, a_in, load_sem.at[0])
    load_b = pltpu.make_async_copy(b_hbm, b_all.at[:, 0:256], load_sem.at[1])
    load_t = pltpu.make_async_copy(t_hbm, t_all.at[core, ab], load_sem.at[2])
    loads_small = [
        pltpu.make_async_copy(src, dst, load_sem.at[3 + i])
        for i, (src, dst) in enumerate(((va_hbm, va_ref), (vb_hbm, vb_ref), (pe_hbm, pe_ref)))
    ]
    for load in (load_a, load_b, load_t, *loads_small):
        load.start()

    row = lax.broadcasted_iota(jnp.int32, (256, 256), 0)
    column = lax.broadcasted_iota(jnp.int32, (256, 256), 1)
    swap = jnp.where(column == (row % 16) * 16 + row // 16, 1.0, 0.0).astype(BF16)

    def block_of(k):
        return ((y + 4) // 2 + k) % 4

    def reorder(k):
        block = block_of(k)
        rows = a_in[:, pl.ds(pl.multiple_of(block * 16, 16), 16), :].reshape(256, 256)
        place = pl.ds(pl.multiple_of(block * 256, 256), 256)
        a_all[place, 0:256] = dot(swap, rows, ((1,), (0,))).astype(BF16)
        return place

    def divisor():
        for load in loads_small:
            load.wait()
        eye = lax.broadcasted_iota(jnp.int32, (16, 16), 0) == lax.broadcasted_iota(jnp.int32, (16, 16), 1)
        va = jnp.sum(jnp.where(eye, jnp.broadcast_to(va_ref[...], (16, 16)), 0.0), axis=1, keepdims=True)
        for b in range(12):
            div_ref[b * 16:(b + 1) * 16, :] = (va + vb_ref[0:1, b:b + 1]) - pe_ref[...]

    def ladder(offset):
        slab = (y + offset + RING) % RING
        left = jnp.concatenate([gath[slab, p] for p in range(PIECES)], axis=1)
        right = t_all[core, pl.ds(2 * slab, 2)].reshape(512, 256)
        return dot(left, right, ((1,), (0,)))

    def early_ladder():
        out_ref[...] = ladder(0)
        for offset in (1, -1, 2, -2, 3, -3):
            out_ref[...] += ladder(offset)

    def core0():
        meet((sibling, z_next[1], z_next[-1], x_far, x_near, x_near_sibling))
        send(1, "b", b_hbm, b_all.at[:, 256:512], sibling, 0)

        def half_rows(half):
            return pl.ds(half * 128, 128)

        t_far = pl.ds(pl.multiple_of((1 - lo) * 128, 128), 128)
        t_near = pl.ds(pl.multiple_of(lo * 128, 128), 128)

        def own(offset):
            return ((z + offset + RING) % RING) * 2 + hi

        def other(offset):
            return ((z + offset + RING) % RING) * 2 + 1 - hi

        def first(col):
            src = t_hbm if col == 0 else t_all.at[1, ab]
            for halves in ((0, 1), (1, 0)):
                for s, half in zip((1, -1), halves):
                    rows = half_rows(half)
                    send(0, ("z", s, 0, half, col), src.at[rows], t_all.at[col, ab, rows], z_next[s], 2)
                if halves == (0, 1):
                    send(0, ("far", 0, col), src.at[t_far], t_all.at[col, ab, t_far], x_far, 3)

        def z_arrived(s, stage, half):
            slab, rows = own(-s * (stage + 1)), half_rows(half)
            if stage == 0:
                for col in range(2):
                    arrived(0, ("z", s, 0, half, col), t_all.at[col, slab, rows])
            else:
                arrived(0, ("z", s, stage, half), t_all.at[:, slab, rows])
            if stage < (3 if half == T_LONG[s] else 2):
                ref = t_all.at[:, slab, rows]
                send(0, ("z", s, stage + 1, half), ref, ref, z_next[s], 2)

        def spread(offset):
            slab = own(offset)
            ref = t_all.at[:, slab] if offset == 4 else t_all.at[:, slab, t_far]
            send(0, ("far", offset), ref, ref, x_far, 3)
            send(1, "t", t_all.at[1, slab], t_all.at[1, slab], sibling, 5)

        def near(offset):
            slab = other(offset)
            if offset == 0:
                for col in range(2):
                    arrived(0, ("far", 0, col), t_all.at[col, slab, t_near])
            else:
                arrived(0, ("far", offset), t_all.at[:, slab, t_near])
            ref0, ref1 = t_all.at[0, slab, t_near], t_all.at[1, slab, t_near]
            send(0, "near", ref0, ref0, x_near, 4)
            send(1, "t", ref1, ref1, x_near_sibling, 4)
            send(1, "t", ref1, ref1, sibling, 6)

        first(0)
        load_a.wait()
        for k in range(4):
            place = reorder(k)
            send(1, ("a", k), a_all.at[place, 0:256], a_all.at[place, 256:512], sibling, 1)
        arrived(0, "t", t_all.at[1, ab])
        first(1)
        divisor()
        load_b.wait()
        load_t.wait()
        for stage in range(4):
            for s in (1, -1):
                z_arrived(s, stage, T_LONG[s])
            if stage < 3:
                for s in (1, -1):
                    z_arrived(s, stage, 1 - T_LONG[s])
                    spread(-s * (stage + 1))
            else:
                spread(4)
            for offset in ((0,), (-1, 1), (-2, 2), (-3, 3))[stage]:
                near(offset)
        slab = other(4)
        arrived(0, ("far", 4), t_all.at[:, slab])
        send(1, "t", t_all.at[1, slab], t_all.at[1, slab], sibling, 7)
        arrived(0, "near", t_all.at[0, 0:7, 0:128])

        arrived(0, "g early", gath.at[0:7])
        early_ladder()
        arrived(0, "g last", gath.at[0])
        out_ref[...] += ladder(4)

        sent(0, b_all.at[:, 0:256])
        sent(1, a_all.at[:, 0:256])
        sent(2, t_all.at[0, 0:14])
        sent(3, t_all.at[0, 0:9])
        sent(4, t_all.at[0, 0:7])
        sent(5, t_all.at[0, 0:7])
        sent(6, t_all.at[0, 0:7, 0:128])
        sent(7, t_all.at[0, 0])

    def core1():
        meet((sibling, y_next[1], y_next[-1], x_near_sibling))
        send(0, "t", t_hbm, t_all.at[1, ab], sibling, 0)
        load_a.wait()
        for k in range(4):
            reorder(k)
        load_b.wait()
        arrived(1, "b", b_all.at[:, 256:512])
        for k in range(4):
            arrived(1, ("a", k), a_all.at[pl.ds(pl.multiple_of(block_of(k) * 256, 256), 256), 256:512])

        def chunk(offset):
            rows = pl.ds(pl.multiple_of(((y + offset + RING) % RING) * 128, 128), 128)
            part[rows, :] = dot(a_all[rows, :], b_all[...], ((1,), (1,)))

        slots = {}

        def own_part(offset, piece):
            chip = (y + offset + RING) % RING
            return part[pl.ds(pl.multiple_of(chip * 128 + piece * 32, 32), 32), :]

        def received(s, stage, piece):
            slot = slots[s, stage, piece]
            arrived(1, ("rs", s, stage, piece), rs_in.at[slot])
            return rs_in[slot].astype(F32)

        def rs_send(s, stage, piece):
            value = own_part(s * ((4 if piece in LONG[s] else 3) - stage), piece)
            if stage:
                value = value + received(s, stage - 1, piece)
            slot = slots.setdefault((s, stage, piece), len(slots))
            rs_out[slot] = value.astype(BF16)
            send(1, ("rs", s, stage, piece), rs_out.at[slot], rs_in.at[slot], y_next[s], 1)

        chunk(4)
        for s, piece in rotation(LONG):
            rs_send(s, 0, piece)
        chunk(3)
        chunk(-3)
        for s, piece in rotation(SHORT):
            rs_send(s, 0, piece)
        chunk(2)
        chunk(-2)
        for stage in (1, 2, 3):
            for s, piece in rotation(LONG):
                rs_send(s, stage, piece)
            if stage < 3:
                for s, piece in rotation(SHORT):
                    rs_send(s, stage, piece)
            if stage == 1:
                chunk(1)
                chunk(-1)
                chunk(0)

        def slab_of(offset):
            return (y + offset + RING) % RING

        def g_send(s, stage, piece):
            ref = gath.at[slab_of(-s * stage), piece]
            send(1, ("g", s, stage, piece), ref, ref, y_next[s], 2)

        def g_arrived(s, stage, piece):
            arrived(1, ("g", s, stage, piece), gath.at[slab_of(-s * (stage + 1)), piece])
            if stage < (3 if piece in LONG[s] else 2):
                g_send(s, stage + 1, piece)

        def g_hand(offset):
            ref = gath.at[slab_of(offset)]
            send(0, "g last" if offset == 4 else "g early", ref, ref, sibling, 3)

        for _, piece in rotation(LONG):
            value = own_part(0, piece)
            for s in (1, -1):
                value = value + received(s, 3 if piece in LONG[s] else 2, piece)
            for b in range(12):
                block = jnp.concatenate([value[c * 16:(c + 1) * 16, b * 64:(b + 1) * 64] for c in range(2)], axis=1)
                gath[y, piece, b * 16:(b + 1) * 16, :] = block.astype(BF16)
            for s in (1, -1):
                g_send(s, 0, piece)
        g_hand(0)
        for stage in range(3):
            for s, piece in rotation(LONG):
                g_arrived(s, stage, piece)
            for s, piece in rotation(SHORT):
                g_arrived(s, stage, piece)
            for s in (1, -1):
                g_hand(-s * (stage + 1))
        divisor()
        load_t.wait()
        arrived(1, "t", t_all.at[1, 0:15])
        early_ladder()
        for s, piece in rotation(LONG):
            g_arrived(s, 3, piece)
        g_hand(4)
        out_ref[...] += ladder(4)

        sent(0, t_all.at[1, 0])
        sent(1, rs_out)
        sent(2, gath.at[0:7])
        sent(3, gath)

    pl.when(core == 0)(core0)
    pl.when(core == 1)(core1)
    assert max(map(len, numbers)) <= N_RECV


def shards(cholesky_a, cholesky_b, amplitudes, other_terms, virtual_a, virtual_b, pair_energy):
    hbm = pl.BlockSpec(memory_space=pltpu.HBM)
    vmem = pl.BlockSpec(memory_space=pltpu.VMEM)
    result = jax.ShapeDtypeStruct((192, 256), F32)
    ladder, divisor = pl.pallas_call(
        kernel,
        out_shape=(result, result),
        in_specs=[hbm] * 6,
        out_specs=(vmem, vmem),
        scratch_shapes=[
            pltpu.VMEM((1, 16), F32),
            pltpu.VMEM((1, 12), F32),
            pltpu.VMEM((1, 256), F32),
            pltpu.VMEM((16, 64, 256), BF16),
            pltpu.VMEM((1024, 512), BF16),
            pltpu.VMEM((768, 512), BF16),
            pltpu.VMEM((1024, 768), F32),
            pltpu.VMEM((28, 32, 768), BF16),
            pltpu.VMEM((28, 32, 768), BF16),
            pltpu.VMEM((8, PIECES, 192, 128), BF16),
            pltpu.VMEM((2, 16, 256, 256), BF16),
            pltpu.SemaphoreType.DMA((N_SEND,)),
            pltpu.SemaphoreType.DMA((N_RECV,)),
            pltpu.SemaphoreType.DMA((6,)),
        ],
        compiler_params=pltpu.CompilerParams(
            collective_id=0, has_side_effects=True, vmem_limit_bytes=40 * 2**20
        ),
        cost_estimate=pl.CostEstimate(flops=2 * 1024 * 512 * 768 + 2 * 192 * 4096 * 256, bytes_accessed=2**21, transcendentals=0),
    )(
        *(
            pltpu.with_memory_space_constraint(operand, pltpu.HBM)
            for operand in (
                cholesky_a, cholesky_b.reshape(768, 256), amplitudes.reshape(256, 256),
                virtual_a.reshape(1, 16), virtual_b.reshape(1, 12), pair_energy.reshape(1, 256),
            )
        )
    )
    residual = other_terms + ladder.reshape(12, 16, 256).transpose(1, 0, 2)
    return (residual, residual / divisor.reshape(12, 16, 256).transpose(1, 0, 2))


def solution(mesh):
    return jax.shard_map(
        shards,
        mesh=mesh,
        in_specs=(
            P(("rep", "ab"), None, "ij"),
            P("rep", None, "ij"),
            P("ab", None, "ij"),
            P(("rep", "ab"), None, "ij"),
            P(("rep", "ab")),
            P("rep"),
            P("ij"),
        ),
        out_specs=(P(("rep", "ab"), None, "ij"), P(("rep", "ab"), None, "ij")),
        check_vma=False,
    )
```

time: 247 us -> 42.6 us (0.17); the launches traced: 244 us -> 42.5 us
  waiting for transfers between devices: 209 us -> 0 us
  Pallas kernels: 0 us -> 41 us
  matrix products: 16.9 us -> 0 us
  between operations: 13.8 us -> 0.66 us
  local copies, waits for them, and re-layouts: 4.07 us -> 0.01 us
    all_gather x3 -> x0, waiting for transfers between devices: 207 us -> none  [the longest x1 72.5 us: shards(): lax.all_gather(amplitudes, 'ab', axis=0, tiled=True)]
    pallas_call x0 -> x1, Pallas kernels: none -> 41 us  [shards(): pl.pallas_call(kernel, out_shape=(result, result), in_specs=[hbm] * 6, ou...]
    dot_general x2 -> x0, matrix products: 16.9 us -> none  [the longest x1 11 us: shards(): lax.dot_general(left.reshape(a_rows * c_count, left.shape[2]), right.resh...]
    reshape x1 -> x0, local copies, waits for them, and re-layouts: 3.3 us -> none  [shards(): summed.astype(jnp.bfloat16).reshape(a_rows, c_count, b_rows, d_count)]
  transfers between devices with their start and end apart: 3 -> 0, of which waited for: 3 -> 0; matrix products, arithmetic and copies ran while one was open for 6% -> 0% of each run, Pallas kernels for 0% -> 0%
where the time goes in v2:
time: 42.6 us; the launch traced here: 42.5 us
  Pallas kernels  41 us (96%)
  other arithmetic  0.79 us (2%)
  between operations  0.66 us (2%)
    pallas_call x1, Pallas kernels, shards(): pl.pallas_call(kernel, out_shape=(result, result), in_specs=[hbm] * 6, ou...  41 us

profile of v2, /device:TPU:1, one launch (start us, length us, event | category | flops | bytes accessed | tf_op | source)
XLA Modules:
  0.0 42.5 jit_solution(14664105645077876628)
XLA Ops:
  0.6 0.0 copy-start
  0.6 41.0 %shard_map.86 = (f32[192,256]{1,0:T(8,128)S(1)}, f32[192,256]{1,0:T(8,128)S(1)}) custom-call(bf16[16,64,256]{2,1,0:T(8,128)(2,1)} %a_hbm.1, bf16[768,256]{1,0:T(8,128)(2,1)} %bitcast.13, bf16[256,256]{1,0:T(8,128)(2,1)} %bitcast.14, f32[1,16]{1,0:T(1,128)} %bitcast.16, f32[1,12]{1,0:T(1,128)} %bitcast.17, f32[1,256]{1,0:T(1,128)} %bitcast.15), custom_call_target="tpu_custom_call" | custom-call | flops 1207959552 | bytes 2097152 | tf_op jit(solution)/shard_map/pallas_call | solution.py:315
  41.7 0.0 copy-done
  41.7 0.8 %fusion = (f32[16,12,256]{2,0,1:T(8,128)}, f32[16,12,256]{2,0,1:T(8,128)}) fusion(f32[16,12,256]{2,0,1:T(8,128)S(1)} %bitcast.12, f32[16,12,256]{2,0,1:T(8,128)S(1)} %copy-done, f32[16,12,256]{2,0,1:T(8,128)S(1)} %bitcast.11), kind=kLoop, calls=%fused_computation | loop fusion | flops 98304 | bytes 983040 | tf_op jit(solution)/shard_map/div | solution.py:350
Async XLA Ops:
  0.6 41.0 %copy-start = (f32[16,12,256]{2,0,1:T(8,128)S(1)}, f32[16,12,256]{2,0,1:T(8,128)}, u32[]{:S(2)}) copy-start(f32[16,12,256]{2,0,1:T(8,128)} %param.10) | copy-start | bytes 589828

commit v3 on v2

--- a/solution.py
+++ b/solution.py
@@ -11,7 +11,6 @@
 PIECES = 4
 LONG = {1: (0, 1), -1: (2, 3)}
 SHORT = {1: (2, 3), -1: (0, 1)}
-T_LONG = {1: 0, -1: 1}
 N_RECV, N_SEND = 68, 8
 
 
@@ -25,13 +24,13 @@
 
 def kernel(a_hbm, b_hbm, t_hbm, va_hbm, vb_hbm, pe_hbm, out_ref, div_ref,
            va_ref, vb_ref, pe_ref, a_in, a_all, b_all, part, rs_in, rs_out, gath, t_all,
-           send_sem, recv_sem, load_sem):
+           send_sem, recv_sem, load_sem, go_sem, ready_sem):
     ab, ij, lo = lax.axis_index("ab"), lax.axis_index("ij"), lax.axis_index("rep")
     z, hi = ab // 2, ab % 2
     y, core = ij // 2, ij % 2
     sibling = (ab, y * 2 + 1 - core, lo)
     y_next = {s: (ab, ((y + s + RING) % RING) * 2 + core, lo) for s in (1, -1)}
-    z_next = {s: (((z + s + RING) % RING) * 2 + hi, ij, lo) for s in (1, -1)}
+    z_hop = {s: (((z + s + RING) % RING) * 2 + hi, ij, lo) for s in (1, -1)}
     x_far = (z * 2 + 1 - hi, ij, 1 - lo)
     x_near = (ab, ij, 1 - lo)
     x_near_sibling = (ab, y * 2 + 1 - core, 1 - lo)
@@ -58,12 +57,6 @@
             src_ref=ref, dst_ref=ref, send_sem=send_sem.at[group], recv_sem=recv_sem.at[0],
             device_id=sibling, device_id_type=MESH,
         ).wait_send()
-
-    def meet(friends):
-        barrier = pltpu.get_barrier_semaphore()
-        for friend in friends:
-            pl.semaphore_signal(barrier, inc=1, device_id=friend, device_id_type=MESH)
-        pl.semaphore_wait(barrier, len(friends))
 
     load_a = pltpu.make_async_copy(a_hbm, a_in, load_sem.at[0])
     load_b = pltpu.make_async_copy(b_hbm, b_all.at[:, 0:256], load_sem.at[1])
@@ -72,8 +65,14 @@
         pltpu.make_async_copy(src, dst, load_sem.at[3 + i])
         for i, (src, dst) in enumerate(((va_hbm, va_ref), (vb_hbm, vb_ref), (pe_hbm, pe_ref)))
     ]
-    for load in (load_a, load_b, load_t, *loads_small):
-        load.start()
+
+    barrier = pltpu.get_barrier_semaphore()
+
+    def enter(friends):
+        for friend in friends:
+            pl.semaphore_signal(barrier, inc=1, device_id=friend, device_id_type=MESH)
+        for load in (load_a, load_b, load_t, *loads_small):
+            load.start()
 
     row = lax.broadcasted_iota(jnp.int32, (256, 256), 0)
     column = lax.broadcasted_iota(jnp.int32, (256, 256), 1)
@@ -109,14 +108,18 @@
             out_ref[...] += ladder(offset)
 
     def core0():
-        meet((sibling, z_next[1], z_next[-1], x_far, x_near, x_near_sibling))
+        friends = (*z_hop.values(), x_far, x_near)
+        enter((sibling, *friends))
+        load_a.wait()
+        places = [reorder(k) for k in range(4)]
+        pl.semaphore_wait(go_sem, 1)
         send(1, "b", b_hbm, b_all.at[:, 256:512], sibling, 0)
 
-        def half_rows(half):
-            return pl.ds(half * 128, 128)
-
-        t_far = pl.ds(pl.multiple_of((1 - lo) * 128, 128), 128)
-        t_near = pl.ds(pl.multiple_of(lo * 128, 128), 128)
+        def rows_of(piece):
+            return pl.ds(piece * 64, 64)
+
+        def rows_x(pair, side):
+            return pl.ds(pl.multiple_of(pair * 128 + side * 64, 64), 64)
 
         def own(offset):
             return ((z + offset + RING) % RING) * 2 + hi
@@ -126,66 +129,65 @@
 
         def first(col):
             src = t_hbm if col == 0 else t_all.at[1, ab]
-            for halves in ((0, 1), (1, 0)):
-                for s, half in zip((1, -1), halves):
-                    rows = half_rows(half)
-                    send(0, ("z", s, 0, half, col), src.at[rows], t_all.at[col, ab, rows], z_next[s], 2)
-                if halves == (0, 1):
-                    send(0, ("far", 0, col), src.at[t_far], t_all.at[col, ab, t_far], x_far, 3)
-
-        def z_arrived(s, stage, half):
-            slab, rows = own(-s * (stage + 1)), half_rows(half)
-            if stage == 0:
-                for col in range(2):
-                    arrived(0, ("z", s, 0, half, col), t_all.at[col, slab, rows])
-            else:
-                arrived(0, ("z", s, stage, half), t_all.at[:, slab, rows])
-            if stage < (3 if half == T_LONG[s] else 2):
-                ref = t_all.at[:, slab, rows]
-                send(0, ("z", s, stage + 1, half), ref, ref, z_next[s], 2)
-
-        def spread(offset):
-            slab = own(offset)
-            ref = t_all.at[:, slab] if offset == 4 else t_all.at[:, slab, t_far]
-            send(0, ("far", offset), ref, ref, x_far, 3)
-            send(1, "t", t_all.at[1, slab], t_all.at[1, slab], sibling, 5)
-
-        def near(offset):
-            slab = other(offset)
-            if offset == 0:
-                for col in range(2):
-                    arrived(0, ("far", 0, col), t_all.at[col, slab, t_near])
-            else:
-                arrived(0, ("far", offset), t_all.at[:, slab, t_near])
-            ref0, ref1 = t_all.at[0, slab, t_near], t_all.at[1, slab, t_near]
+            for pieces in (LONG, SHORT):
+                for s, piece in rotation(pieces):
+                    rows = rows_of(piece)
+                    send(0, ("z", s, 1, piece), src.at[rows], t_all.at[col, ab, rows], z_hop[s], 2)
+                if pieces is LONG:
+                    for pair in range(2):
+                        rows = rows_x(pair, 1 - lo)
+                        send(0, ("far", 0, pair), src.at[rows], t_all.at[col, ab, rows], x_far, 3)
+
+        def z_arrived(s, distance, piece):
+            slab, rows = own(-s * distance), rows_of(piece)
+            ref = t_all.at[:, slab, rows]
+            arrived(0, ("z", s, distance, piece), ref)
+            if distance < (4 if piece in LONG[s] else 3):
+                send(0, ("z", s, distance + 1, piece), ref, ref, z_hop[s], 2)
+            send(1, "t", t_all.at[1, slab, rows], t_all.at[1, slab, rows], sibling, 5)
+
+        def z_pair(s, distance, pieces):
+            offset = 4 if distance == 4 else -s * distance
+            pair = pieces[s][0] // 2
+            rows = pl.ds(pair * 128, 128) if offset == 4 else rows_x(pair, 1 - lo)
+            ref = t_all.at[:, own(offset), rows]
+            send(0, ("far", offset, pair), ref, ref, x_far, 3)
+
+        def near(offset, pair):
+            slab, rows = other(offset), rows_x(pair, lo)
+            arrived(0, ("far", offset, pair), t_all.at[:, slab, rows])
+            ref0, ref1 = t_all.at[0, slab, rows], t_all.at[1, slab, rows]
             send(0, "near", ref0, ref0, x_near, 4)
             send(1, "t", ref1, ref1, x_near_sibling, 4)
             send(1, "t", ref1, ref1, sibling, 6)
 
+        for k, place in enumerate(places):
+            send(1, "a rest" if k else "a first", a_all.at[place, 0:256], a_all.at[place, 256:512], sibling, 1)
+        pl.semaphore_wait(barrier, len(friends))
         first(0)
-        load_a.wait()
-        for k in range(4):
-            place = reorder(k)
-            send(1, ("a", k), a_all.at[place, 0:256], a_all.at[place, 256:512], sibling, 1)
+        pl.semaphore_signal(ready_sem, inc=1, device_id=x_near, device_id_type=MESH)
         arrived(0, "t", t_all.at[1, ab])
         first(1)
-        divisor()
         load_b.wait()
         load_t.wait()
-        for stage in range(4):
-            for s in (1, -1):
-                z_arrived(s, stage, T_LONG[s])
-            if stage < 3:
+        divisor()
+        for distance in (1, 2, 3, 4):
+            for pieces in (LONG, SHORT) if distance < 4 else (LONG,):
+                for s, piece in rotation(pieces):
+                    z_arrived(s, distance, piece)
                 for s in (1, -1):
-                    z_arrived(s, stage, 1 - T_LONG[s])
-                    spread(-s * (stage + 1))
+                    z_pair(s, distance, pieces)
+            if distance == 1:
+                pl.semaphore_wait(ready_sem, 1)
+                for pair in range(2):
+                    near(0, pair)
             else:
-                spread(4)
-            for offset in ((0,), (-1, 1), (-2, 2), (-3, 3))[stage]:
-                near(offset)
-        slab = other(4)
-        arrived(0, ("far", 4), t_all.at[:, slab])
-        send(1, "t", t_all.at[1, slab], t_all.at[1, slab], sibling, 7)
+                for s, pair in ((1, 0), (-1, 1), (1, 1), (-1, 0)):
+                    near(-s * (distance - 1), pair)
+        for pair in range(2):
+            slab, rows = other(4), pl.ds(pair * 128, 128)
+            arrived(0, ("far", 4, pair), t_all.at[:, slab, rows])
+            send(1, "t", t_all.at[1, slab, rows], t_all.at[1, slab, rows], sibling, 7)
         arrived(0, "near", t_all.at[0, 0:7, 0:128])
 
         arrived(0, "g early", gath.at[0:7])
@@ -203,19 +205,18 @@
         sent(7, t_all.at[0, 0])
 
     def core1():
-        meet((sibling, y_next[1], y_next[-1], x_near_sibling))
+        enter(y_next.values())
+        pl.semaphore_wait(barrier, 3)
+        pl.semaphore_signal(go_sem, inc=1, device_id=sibling, device_id_type=MESH)
         send(0, "t", t_hbm, t_all.at[1, ab], sibling, 0)
-        load_a.wait()
-        for k in range(4):
-            reorder(k)
-        load_b.wait()
-        arrived(1, "b", b_all.at[:, 256:512])
-        for k in range(4):
-            arrived(1, ("a", k), a_all.at[pl.ds(pl.multiple_of(block_of(k) * 256, 256), 256), 256:512])
-
-        def chunk(offset):
-            rows = pl.ds(pl.multiple_of(((y + offset + RING) % RING) * 128, 128), 128)
-            part[rows, :] = dot(a_all[rows, :], b_all[...], ((1,), (1,)))
+        def chunk_rows(offset):
+            return pl.ds(pl.multiple_of(((y + offset + RING) % RING) * 128, 128), 128)
+
+        def add_sibling(*offsets):
+            left = jnp.concatenate([a_all[chunk_rows(offset), 256:512] for offset in offsets], axis=0)
+            product = dot(left, b_all[:, 256:512], ((1,), (1,)))
+            for i, offset in enumerate(offsets):
+                part[chunk_rows(offset), :] += product[i * 128:(i + 1) * 128]
 
         slots = {}
 
@@ -236,25 +237,31 @@
             rs_out[slot] = value.astype(BF16)
             send(1, ("rs", s, stage, piece), rs_out.at[slot], rs_in.at[slot], y_next[s], 1)
 
-        chunk(4)
-        for s, piece in rotation(LONG):
-            rs_send(s, 0, piece)
-        chunk(3)
-        chunk(-3)
-        for s, piece in rotation(SHORT):
-            rs_send(s, 0, piece)
-        chunk(2)
-        chunk(-2)
-        for stage in (1, 2, 3):
-            for s, piece in rotation(LONG):
+        def rs_stage(stage, pieces):
+            for s, piece in rotation(pieces):
                 rs_send(s, stage, piece)
-            if stage < 3:
-                for s, piece in rotation(SHORT):
-                    rs_send(s, stage, piece)
-            if stage == 1:
-                chunk(1)
-                chunk(-1)
-                chunk(0)
+
+        load_a.wait()
+        for k in range(4):
+            reorder(k)
+        load_b.wait()
+        for rows in (slice(0, 512), slice(512, 1024)):
+            part[rows, :] = dot(a_all[rows, 0:256], b_all[:, 0:256], ((1,), (1,)))
+        arrived(1, "b", b_all.at[:, 256:512])
+        arrived(1, "a first", a_all.at[0:256, 256:512])
+        add_sibling(4)
+        rs_stage(0, LONG)
+        arrived(1, "a rest", a_all.at[0:768, 256:512])
+        add_sibling(3, -3)
+        rs_stage(0, SHORT)
+        add_sibling(2, -2)
+        rs_stage(1, LONG)
+        rs_stage(1, SHORT)
+        add_sibling(1, -1)
+        rs_stage(2, LONG)
+        rs_stage(2, SHORT)
+        add_sibling(0)
+        rs_stage(3, LONG)
 
         def slab_of(offset):
             return (y + offset + RING) % RING
@@ -264,38 +271,38 @@
             send(1, ("g", s, stage, piece), ref, ref, y_next[s], 2)
 
         def g_arrived(s, stage, piece):
-            arrived(1, ("g", s, stage, piece), gath.at[slab_of(-s * (stage + 1)), piece])
+            offset = -s * (stage + 1)
+            arrived(1, ("g", s, stage, piece), gath.at[slab_of(offset), piece])
             if stage < (3 if piece in LONG[s] else 2):
                 g_send(s, stage + 1, piece)
-
-        def g_hand(offset):
-            ref = gath.at[slab_of(offset)]
-            send(0, "g last" if offset == 4 else "g early", ref, ref, sibling, 3)
-
-        for _, piece in rotation(LONG):
+            g_hand(offset, piece)
+
+        def g_hand(offset, piece):
+            ref = gath.at[slab_of(offset), piece]
+            send(0, "g last" if abs(offset) == 4 else "g early", ref, ref, sibling, 3)
+
+        for way, piece in rotation(LONG):
             value = own_part(0, piece)
             for s in (1, -1):
                 value = value + received(s, 3 if piece in LONG[s] else 2, piece)
             for b in range(12):
                 block = jnp.concatenate([value[c * 16:(c + 1) * 16, b * 64:(b + 1) * 64] for c in range(2)], axis=1)
                 gath[y, piece, b * 16:(b + 1) * 16, :] = block.astype(BF16)
-            for s in (1, -1):
-                g_send(s, 0, piece)
-        g_hand(0)
+            g_send(way, 0, piece)
+        for s, piece in rotation(SHORT):
+            g_send(s, 0, piece)
+        for piece in range(PIECES):
+            g_hand(0, piece)
         for stage in range(3):
-            for s, piece in rotation(LONG):
-                g_arrived(s, stage, piece)
-            for s, piece in rotation(SHORT):
-                g_arrived(s, stage, piece)
-            for s in (1, -1):
-                g_hand(-s * (stage + 1))
+            for pieces in (LONG, SHORT):
+                for s, piece in rotation(pieces):
+                    g_arrived(s, stage, piece)
         divisor()
         load_t.wait()
         arrived(1, "t", t_all.at[1, 0:15])
         early_ladder()
         for s, piece in rotation(LONG):
             g_arrived(s, 3, piece)
-        g_hand(4)
         out_ref[...] += ladder(4)
 
         sent(0, t_all.at[1, 0])
@@ -303,8 +310,8 @@
         sent(2, gath.at[0:7])
         sent(3, gath)
 
+    pl.when(core == 1)(core1)
     pl.when(core == 0)(core0)
-    pl.when(core == 1)(core1)
     assert max(map(len, numbers)) <= N_RECV
 
 
@@ -332,6 +339,8 @@
             pltpu.SemaphoreType.DMA((N_SEND,)),
             pltpu.SemaphoreType.DMA((N_RECV,)),
             pltpu.SemaphoreType.DMA((6,)),
+            pltpu.SemaphoreType.REGULAR,
+            pltpu.SemaphoreType.REGULAR,
         ],
         compiler_params=pltpu.CompilerParams(
             collective_id=0, has_side_effects=True, vmem_limit_bytes=40 * 2**20

time: 42.6 us -> 40.5 us (0.951)
  Pallas kernels: 41 us -> 38.9 us
    pallas_call x1, Pallas kernels: 41 us -> 38.9 us  [shards(): pl.pallas_call(kernel, out_shape=(result, result), in_specs=[hbm] * 6, ou...]
where the time goes in v3:
time: 40.5 us; the launch traced here: 40.4 us
  Pallas kernels  38.9 us (96%)
  other arithmetic  0.79 us (2%)
  between operations  0.66 us (2%)
    pallas_call x1, Pallas kernels, shards(): pl.pallas_call(kernel, out_shape=(result, result), in_specs=[hbm] * 6, ou...  38.9 us

profile of v3, /device:TPU:1, one launch (start us, length us, event | category | flops | bytes accessed | tf_op | source)
XLA Modules:
  0.0 40.4 jit_solution(8004509340906958231)
XLA Ops:
  0.6 0.0 copy-start
  0.6 38.9 %shard_map.86 = (f32[192,256]{1,0:T(8,128)S(1)}, f32[192,256]{1,0:T(8,128)S(1)}) custom-call(bf16[16,64,256]{2,1,0:T(8,128)(2,1)} %a_hbm.1, bf16[768,256]{1,0:T(8,128)(2,1)} %bitcast.13, bf16[256,256]{1,0:T(8,128)(2,1)} %bitcast.14, f32[1,16]{1,0:T(1,128)} %bitcast.16, f32[1,12]{1,0:T(1,128)} %bitcast.17, f32[1,256]{1,0:T(1,128)} %bitcast.15), custom_call_target="tpu_custom_call" | custom-call | flops 1207959552 | bytes 2097152 | tf_op jit(solution)/shard_map/pallas_call | solution.py:322
  39.6 0.0 copy-done
  39.6 0.8 %fusion = (f32[16,12,256]{2,0,1:T(8,128)}, f32[16,12,256]{2,0,1:T(8,128)}) fusion(f32[16,12,256]{2,0,1:T(8,128)S(1)} %bitcast.12, f32[16,12,256]{2,0,1:T(8,128)S(1)} %copy-done, f32[16,12,256]{2,0,1:T(8,128)S(1)} %bitcast.11), kind=kLoop, calls=%fused_computation | loop fusion | flops 98304 | bytes 983040 | tf_op jit(solution)/shard_map/div | solution.py:359
Async XLA Ops:
  0.6 39.0 %copy-start = (f32[16,12,256]{2,0,1:T(8,128)S(1)}, f32[16,12,256]{2,0,1:T(8,128)}, u32[]{:S(2)}) copy-start(f32[16,12,256]{2,0,1:T(8,128)} %param.10) | copy-start | bytes 589828

commit v4 on v3

v4 whole, which is shorter than its diff:
```python
import jax
import jax.numpy as jnp
from jax import lax
from jax.experimental import pallas as pl
from jax.experimental.pallas import tpu as pltpu
from jax.sharding import PartitionSpec as P

MESH = pl.DeviceIdType.MESH
BF16, F32 = jnp.bfloat16, jnp.float32
RING = 8
PIECES = 4
LONG = {1: (0, 1), -1: (2, 3)}
SHORT = {1: (2, 3), -1: (0, 1)}
N_RECV, N_SEND = 50, 7


SLOTS = {
    key: i for i, key in enumerate(
        (s, stage, piece) for s in (1, -1) for stage in range(4) for piece in LONG[s] + (SHORT[s] if stage < 3 else ())
    )
}


def dot(a, b, dims):
    return lax.dot_general(a, b, (dims, ((), ())), preferred_element_type=F32)


def rotation(pieces, ways=(1, -1)):
    return [(s, pieces[s][i]) for i in range(PIECES // 2) for s in ways]


def kernel(a_hbm, b_hbm, t_hbm, va_hbm, vb_hbm, pe_hbm, out_ref, div_ref,
           va_ref, vb_ref, pe_ref, a_in, a_all, b_all, part, part_0, rs_in, rs_out, gath, t_all,
           send_sem, recv_sem, load_sem, go_sem, ready_sem):
    ab, ij, lo = lax.axis_index("ab"), lax.axis_index("ij"), lax.axis_index("rep")
    z, hi = ab // 2, ab % 2
    y, core = ij // 2, ij % 2
    sibling = (ab, y * 2 + 1 - core, lo)
    y_next = {s: (ab, ((y + s + RING) % RING) * 2 + core, lo) for s in (1, -1)}
    z_hop = {s: (((z + s + RING) % RING) * 2 + hi, ij, lo) for s in (1, -1)}
    x_far = (z * 2 + 1 - hi, ij, 1 - lo)
    x_near = (ab, ij, 1 - lo)
    x_near_sibling = (ab, y * 2 + 1 - core, 1 - lo)

    numbers = ({}, {})

    def recv_of(to, name):
        if name[0] == "g":
            name = ("rs", *name[1:])
        return recv_sem.at[numbers[to].setdefault(name, len(numbers[to]))]

    def send(to, name, src, dst, device, group):
        pltpu.make_async_remote_copy(
            src_ref=src, dst_ref=dst, send_sem=send_sem.at[group], recv_sem=recv_of(to, name),
            device_id=device, device_id_type=MESH,
        ).start()

    def arrived(to, name, ref):
        pltpu.make_async_remote_copy(
            src_ref=ref, dst_ref=ref, send_sem=send_sem.at[0], recv_sem=recv_of(to, name),
            device_id=sibling, device_id_type=MESH,
        ).wait_recv()

    def sent(group, ref):
        pltpu.make_async_remote_copy(
            src_ref=ref, dst_ref=ref, send_sem=send_sem.at[group], recv_sem=recv_sem.at[0],
            device_id=sibling, device_id_type=MESH,
        ).wait_send()

    load_a = pltpu.make_async_copy(a_hbm, a_in, load_sem.at[0])
    load_b = pltpu.make_async_copy(b_hbm, b_all, load_sem.at[1])
    load_t = pltpu.make_async_copy(t_hbm, t_all.at[core, ab], load_sem.at[2])
    loads_small = [
        pltpu.make_async_copy(src, dst, load_sem.at[3 + i])
        for i, (src, dst) in enumerate(((va_hbm, va_ref), (vb_hbm, vb_ref), (pe_hbm, pe_ref)))
    ]

    barrier = pltpu.get_barrier_semaphore()

    def enter(friends):
        for friend in friends:
            pl.semaphore_signal(barrier, inc=1, device_id=friend, device_id_type=MESH)
        for load in (load_a, load_b, load_t, *loads_small):
            load.start()

    row = lax.broadcasted_iota(jnp.int32, (256, 256), 0)
    column = lax.broadcasted_iota(jnp.int32, (256, 256), 1)
    swap = jnp.where(column == (row % 16) * 16 + row // 16, 1.0, 0.0).astype(BF16)

    def block_of(k):
        return ((y + 4) // 2 + k) % 4

    def reorder(k):
        block = block_of(k)
        rows = a_in[:, pl.ds(pl.multiple_of(block * 16, 16), 16), :].reshape(256, 256)
        place = pl.ds(pl.multiple_of(block * 256, 256), 256)
        a_all[place, :] = dot(swap, rows, ((1,), (0,))).astype(BF16)

    def chunk_rows(offset):
        return pl.ds(pl.multiple_of(((y + offset + RING) % RING) * 128, 128), 128)

    def products(ref, *offsets):
        left = jnp.concatenate([a_all[chunk_rows(offset), :] for offset in offsets], axis=0)
        value = dot(left, b_all[...], ((1,), (1,))).astype(ref.dtype)
        for i, offset in enumerate(offsets):
            ref[chunk_rows(offset), :] = value[i * 128:(i + 1) * 128]

    def divisor():
        for load in loads_small:
            load.wait()
        eye = lax.broadcasted_iota(jnp.int32, (16, 16), 0) == lax.broadcasted_iota(jnp.int32, (16, 16), 1)
        va = jnp.sum(jnp.where(eye, jnp.broadcast_to(va_ref[...], (16, 16)), 0.0), axis=1, keepdims=True)
        for b in range(12):
            div_ref[b * 16:(b + 1) * 16, :] = (va + vb_ref[0:1, b:b + 1]) - pe_ref[...]

    far_y = (y + 4) % RING
    far_z = jnp.where(z == y, (y + 5) % RING, (z + 4) % RING)
    low, high = jnp.minimum(far_y, far_z), jnp.maximum(far_y, far_z)

    def ladder(slabs):
        total = None
        for slab in slabs:
            left = jnp.concatenate([gath[slab, p] for p in range(PIECES)], axis=1)
            right = t_all[core, pl.ds(2 * slab, 2)].reshape(512, 256)
            product = dot(left, right, ((1,), (0,)))
            total = product if total is None else total + product
        return total

    def early_ladder():
        slabs = []
        for k in range(RING - 2):
            slab = k + jnp.where(k >= low, 1, 0)
            slabs.append(slab + jnp.where(slab >= high, 1, 0))
        out_ref[...] = ladder(slabs)

    def late_ladder():
        out_ref[...] += ladder((far_y, far_z))

    def core0():
        friends = (*z_hop.values(), x_far, x_near)
        enter((sibling, *friends))

        def hand_products(*offsets):
            products(part_0, *offsets)
            if offsets == (4,):
                pl.semaphore_wait(go_sem, 1)
            for offset in offsets:
                ref = part_0.at[chunk_rows(offset)]
                send(1, ("p", offsets[0]), ref, ref, sibling, 0)

        load_a.wait()
        reorder(0)
        load_b.wait()
        hand_products(4)
        for k in (1, 3, 2):
            reorder(k)
        hand_products(3, -3)

        def rows_x(pair, side):
            return pl.ds(pl.multiple_of(pair * 128 + side * 64, 64), 64)

        def rows_of(piece):
            return rows_x(piece // 2, lo if piece % 2 else 1 - lo)

        def own(offset):
            return ((z + offset + RING) % RING) * 2 + hi

        def other(offset):
            return ((z + offset + RING) % RING) * 2 + 1 - hi

        def z_send(s, distance, piece):
            ref = t_all.at[:, own(-s * (distance - 1)), rows_of(piece)]
            send(0, ("z", s, distance, piece), ref, ref, z_hop[s], 2)

        def far_send(offset, piece):
            name = ("far", offset, piece if offset == 4 else piece // 2)
            ref = t_all.at[:, own(offset), rows_of(piece)]
            send(0, name, ref, ref, x_far, 3)

        def z_arrived(s, distance, piece):
            slab, rows = own(-s * distance), rows_of(piece)
            arrived(0, ("z", s, distance, piece), t_all.at[:, slab, rows])
            if distance < (4 if piece in LONG[s] else 3):
                z_send(s, distance + 1, piece)
            if distance == 4:
                far_send(4, piece)
            elif piece % 2 == 0:
                far_send(-s * distance, piece)
            send(1, "t", t_all.at[1, slab, rows], t_all.at[1, slab, rows], sibling, 5)

        def near(offset, pair):
            slab, rows = other(offset), rows_x(pair, lo)
            arrived(0, ("far", offset, pair), t_all.at[:, slab, rows])
            ref0, ref1 = t_all.at[0, slab, rows], t_all.at[1, slab, rows]
            send(0, "near", ref0, ref0, x_near, 4)
            send(1, "t", ref1, ref1, x_near_sibling, 4)
            send(1, "t", ref1, ref1, sibling, 6)

        pl.semaphore_wait(barrier, len(friends))
        pl.semaphore_signal(ready_sem, inc=1, device_id=x_near, device_id_type=MESH)
        load_t.wait()
        arrived(0, "t", t_all.at[1, ab])
        for s, piece in rotation(LONG):
            z_send(s, 1, piece)
        for pair in range(2):
            far_send(0, 2 * pair)
        for s, piece in rotation(SHORT):
            z_send(s, 1, piece)
        hand_products(2, -2)
        hand_products(1, -1)
        hand_products(0)
        divisor()
        for distance in (1, 2, 3, 4):
            for pieces in (LONG, SHORT) if distance < 4 else (LONG,):
                for s, piece in rotation(pieces):
                    z_arrived(s, distance, piece)
            if distance == 1:
                pl.semaphore_wait(ready_sem, 1)
                for pair in range(2):
                    near(0, pair)
            else:
                for s, pair in ((1, 0), (-1, 1), (1, 1), (-1, 0)):
                    near(-s * (distance - 1), pair)
        slab = other(4)
        for _, piece in rotation(LONG):
            rows = rows_x(piece // 2, 1 - lo if piece % 2 else lo)
            arrived(0, ("far", 4, piece), t_all.at[:, slab, rows])
            send(1, "t last", t_all.at[1, slab, rows], t_all.at[1, slab, rows], sibling, 1)
        arrived(0, "near", t_all.at[0, 0:7, 0:128])

        arrived(0, "g early", gath.at[0:7])
        early_ladder()
        arrived(0, "g last", gath.at[0])
        late_ladder()

        sent(0, part_0)
        sent(1, t_all.at[0, 0])
        sent(2, t_all.at[0, 0:14])
        sent(3, t_all.at[0, 0:9])
        sent(4, t_all.at[0, 0:7])
        sent(5, t_all.at[0, 0:7])
        sent(6, t_all.at[0, 0:7, 0:128])

    def core1(ways):
        enter(y_next.values())
        pl.semaphore_wait(barrier, 3)
        pl.semaphore_signal(go_sem, inc=1, device_id=sibling, device_id_type=MESH)
        send(0, "t", t_hbm, t_all.at[1, ab], sibling, 0)

        def own_part(offset, piece):
            chip = (y + offset + RING) % RING
            rows = pl.ds(pl.multiple_of(chip * 128 + piece * 32, 32), 32)
            return part[rows, :] + part_0[rows, :].astype(F32)

        def received(s, stage, piece):
            slot = SLOTS[s, stage, piece]
            arrived(1, ("rs", s, stage, piece), rs_in.at[slot])
            return rs_in[slot].astype(F32)

        def rs_send(s, stage, piece):
            value = own_part(s * ((4 if piece in LONG[s] else 3) - stage), piece)
            if stage:
                value = value + received(s, stage - 1, piece)
            slot = SLOTS[s, stage, piece]
            rs_out[slot] = value.astype(BF16)
            send(1, ("rs", s, stage, piece), rs_out.at[slot], rs_in.at[slot], y_next[s], 1)

        def rs_stage(stage, pieces):
            for s, piece in rotation(pieces, ways):
                rs_send(s, stage, piece)

        load_a.wait()
        for k in range(4):
            reorder(k)
        load_b.wait()
        products(part, 4)
        products(part, 3, -3)
        products(part, 2, -2)
        arrived(1, ("p", 4), part_0.at[0:128])
        rs_stage(0, LONG)
        arrived(1, ("p", 3), part_0.at[0:256])
        rs_stage(0, SHORT)
        products(part, 1, -1)
        products(part, 0)
        rs_stage(1, LONG)
        arrived(1, ("p", 2), part_0.at[0:256])
        rs_stage(1, SHORT)
        rs_stage(2, LONG)
        arrived(1, ("p", 1), part_0.at[0:256])
        rs_stage(2, SHORT)
        rs_stage(3, LONG)
        arrived(1, ("p", 0), part_0.at[0:128])

        def slab_of(offset):
            return (y + offset + RING) % RING

        def g_send(s, stage, piece):
            ref = gath.at[slab_of(-s * stage), piece]
            send(1, ("g", s, stage, piece), ref, ref, y_next[s], 2)

        def g_arrived(s, stage, piece):
            offset = -s * (stage + 1)
            arrived(1, ("g", s, stage, piece), gath.at[slab_of(offset), piece])
            if stage < (3 if piece in LONG[s] else 2):
                g_send(s, stage + 1, piece)
            g_hand(offset, piece)

        def g_hand(offset, piece):
            ref = gath.at[slab_of(offset), piece]
            send(0, "g last" if abs(offset) == 4 else "g early", ref, ref, sibling, 3)

        for way, piece in rotation(LONG, ways):
            value = own_part(0, piece)
            for s in (1, -1):
                value = value + received(s, 3 if piece in LONG[s] else 2, piece)
            for b in range(12):
                block = jnp.concatenate([value[c * 16:(c + 1) * 16, b * 64:(b + 1) * 64] for c in range(2)], axis=1)
                gath[y, piece, b * 16:(b + 1) * 16, :] = block.astype(BF16)
            g_send(way, 0, piece)
        for s, piece in rotation(SHORT, ways):
            g_send(s, 0, piece)
        for piece in range(PIECES):
            g_hand(0, piece)
        for stage in range(3):
            for pieces in (LONG, SHORT):
                for s, piece in rotation(pieces, ways):
                    g_arrived(s, stage, piece)
        divisor()
        load_t.wait()
        for s, piece in rotation(LONG, ways):
            g_arrived(s, 3, piece)
        arrived(1, "t", t_all.at[1, 0:14])
        early_ladder()
        arrived(1, "t last", t_all.at[1, 0])
        late_ladder()

        sent(0, t_all.at[1, 0])
        sent(1, rs_out)
        sent(2, gath.at[0:7])
        sent(3, gath)

    pl.when((core == 1) & (y % 4 < 2))(lambda: core1((-1, 1)))
    pl.when((core == 1) & (y % 4 >= 2))(lambda: core1((1, -1)))
    pl.when(core == 0)(core0)
    assert max(map(len, numbers)) <= N_RECV


def shards(cholesky_a, cholesky_b, amplitudes, other_terms, virtual_a, virtual_b, pair_energy):
    hbm = pl.BlockSpec(memory_space=pltpu.HBM)
    vmem = pl.BlockSpec(memory_space=pltpu.VMEM)
    result = jax.ShapeDtypeStruct((192, 256), F32)
    ladder, divisor = pl.pallas_call(
        kernel,
        out_shape=(result, result),
        in_specs=[hbm] * 6,
        out_specs=(vmem, vmem),
        scratch_shapes=[
            pltpu.VMEM((1, 16), F32),
            pltpu.VMEM((1, 12), F32),
            pltpu.VMEM((1, 256), F32),
            pltpu.VMEM((16, 64, 256), BF16),
            pltpu.VMEM((1024, 256), BF16),
            pltpu.VMEM((768, 256), BF16),
            pltpu.VMEM((1024, 768), F32),
            pltpu.VMEM((1024, 768), BF16),
            pltpu.VMEM((28, 32, 768), BF16),
            pltpu.VMEM((28, 32, 768), BF16),
            pltpu.VMEM((8, PIECES, 192, 128), BF16),
            pltpu.VMEM((2, 16, 256, 256), BF16),
            pltpu.SemaphoreType.DMA((N_SEND,)),
            pltpu.SemaphoreType.DMA((N_RECV,)),
            pltpu.SemaphoreType.DMA((6,)),
            pltpu.SemaphoreType.REGULAR,
            pltpu.SemaphoreType.REGULAR,
        ],
        compiler_params=pltpu.CompilerParams(
            collective_id=0, has_side_effects=True, vmem_limit_bytes=40 * 2**20
        ),
        cost_estimate=pl.CostEstimate(flops=2 * 1024 * 512 * 768 + 2 * 192 * 4096 * 256, bytes_accessed=2**21, transcendentals=0),
    )(
        *(
            pltpu.with_memory_space_constraint(operand, pltpu.HBM)
            for operand in (
                cholesky_a, cholesky_b.reshape(768, 256), amplitudes.reshape(256, 256),
                virtual_a.reshape(1, 16), virtual_b.reshape(1, 12), pair_energy.reshape(1, 256),
            )
        )
    )
    residual = other_terms + ladder.reshape(12, 16, 256).transpose(1, 0, 2)
    return (residual, residual / divisor.reshape(12, 16, 256).transpose(1, 0, 2))


def solution(mesh):
    return jax.shard_map(
        shards,
        mesh=mesh,
        in_specs=(
            P(("rep", "ab"), None, "ij"),
            P("rep", None, "ij"),
            P("ab", None, "ij"),
            P(("rep", "ab"), None, "ij"),
            P(("rep", "ab")),
            P("rep"),
            P("ij"),
        ),
        out_specs=(P(("rep", "ab"), None, "ij"), P(("rep", "ab"), None, "ij")),
        check_vma=False,
    )
```

time: 40.5 us -> 38 us (0.938)
  Pallas kernels: 38.9 us -> 36.4 us
    pallas_call x1, Pallas kernels: 38.9 us -> 36.4 us  [shards(): pl.pallas_call(kernel, out_shape=(result, result), in_specs=[hbm] * 6, ou...]
where the time goes in v4:
time: 38 us; the launch traced here: 37.8 us
  Pallas kernels  36.4 us (96%)
  other arithmetic  0.79 us (2%)
  between operations  0.66 us (2%)
    pallas_call x1, Pallas kernels, shards(): pl.pallas_call(kernel, out_shape=(result, result), in_specs=[hbm] * 6, ou...  36.4 us
    div x1, other arithmetic, shards(): residual / divisor.reshape(12, 16, 256).transpose(1, 0, 2)  0.79 us

profile of v4, /device:TPU:1, one launch (start us, length us, event | category | flops | bytes accessed | tf_op | source)
XLA Modules:
  0.0 37.8 jit_solution(11415931576057625850)
XLA Ops:
  0.6 0.0 copy-start
  0.6 36.4 %shard_map.86 = (f32[192,256]{1,0:T(8,128)S(1)}, f32[192,256]{1,0:T(8,128)S(1)}) custom-call(bf16[16,64,256]{2,1,0:T(8,128)(2,1)} %a_hbm.1, bf16[768,256]{1,0:T(8,128)(2,1)} %bitcast.13, bf16[256,256]{1,0:T(8,128)(2,1)} %bitcast.14, f32[1,16]{1,0:T(1,128)} %bitcast.16, f32[1,12]{1,0:T(1,128)} %bitcast.17, f32[1,256]{1,0:T(1,128)} %bitcast.15), custom_call_target="tpu_custom_call" | custom-call | flops 1207959552 | bytes 2097152 | tf_op jit(solution)/shard_map/pallas_call | solution.py:352
  37.0 0.0 copy-done
  37.1 0.8 %fusion = (f32[16,12,256]{2,0,1:T(8,128)}, f32[16,12,256]{2,0,1:T(8,128)}) fusion(f32[16,12,256]{2,0,1:T(8,128)S(1)} %bitcast.12, f32[16,12,256]{2,0,1:T(8,128)S(1)} %copy-done, f32[16,12,256]{2,0,1:T(8,128)S(1)} %bitcast.11), kind=kLoop, calls=%fused_computation | loop fusion | flops 98304 | bytes 983040 | tf_op jit(solution)/shard_map/div | solution.py:390
Async XLA Ops:
  0.6 36.4 %copy-start = (f32[16,12,256]{2,0,1:T(8,128)S(1)}, f32[16,12,256]{2,0,1:T(8,128)}, u32[]{:S(2)}) copy-start(f32[16,12,256]{2,0,1:T(8,128)} %param.10) | copy-start | bytes 589828

commit v5 on v4

--- a/solution.py
+++ b/solution.py
@@ -11,7 +11,7 @@
 PIECES = 4
 LONG = {1: (0, 1), -1: (2, 3)}
 SHORT = {1: (2, 3), -1: (0, 1)}
-N_RECV, N_SEND = 50, 7
+N_RECV, N_SEND = 49, 7
 
 
 SLOTS = {
@@ -40,12 +40,13 @@
     z_hop = {s: (((z + s + RING) % RING) * 2 + hi, ij, lo) for s in (1, -1)}
     x_far = (z * 2 + 1 - hi, ij, 1 - lo)
     x_near = (ab, ij, 1 - lo)
+    x_far_sibling = (z * 2 + 1 - hi, y * 2 + 1 - core, 1 - lo)
     x_near_sibling = (ab, y * 2 + 1 - core, 1 - lo)
 
     numbers = ({}, {})
 
     def recv_of(to, name):
-        if name[0] == "g":
+        if isinstance(name, tuple) and name[0] == "g":
             name = ("rs", *name[1:])
         return recv_sem.at[numbers[to].setdefault(name, len(numbers[to]))]
 
@@ -87,17 +88,17 @@
     column = lax.broadcasted_iota(jnp.int32, (256, 256), 1)
     swap = jnp.where(column == (row % 16) * 16 + row // 16, 1.0, 0.0).astype(BF16)
 
-    def block_of(k):
-        return ((y + 4) // 2 + k) % 4
-
     def reorder(k):
-        block = block_of(k)
+        block = ((y + 4) // 2 + k) % 4
         rows = a_in[:, pl.ds(pl.multiple_of(block * 16, 16), 16), :].reshape(256, 256)
         place = pl.ds(pl.multiple_of(block * 256, 256), 256)
         a_all[place, :] = dot(swap, rows, ((1,), (0,))).astype(BF16)
 
     def chunk_rows(offset):
         return pl.ds(pl.multiple_of(((y + offset + RING) % RING) * 128, 128), 128)
+
+    def piece_rows(offset, piece):
+        return pl.ds(pl.multiple_of(((y + offset + RING) % RING) * 128 + piece * 32, 32), 32)
 
     def products(ref, *offsets):
         left = jnp.concatenate([a_all[chunk_rows(offset), :] for offset in offsets], axis=0)
@@ -114,8 +115,11 @@
             div_ref[b * 16:(b + 1) * 16, :] = (va + vb_ref[0:1, b:b + 1]) - pe_ref[...]
 
     far_y = (y + 4) % RING
-    far_z = jnp.where(z == y, (y + 5) % RING, (z + 4) % RING)
-    low, high = jnp.minimum(far_y, far_z), jnp.maximum(far_y, far_z)
+    ahead = (far_y - z + 2 + RING) % RING
+    skipped = jnp.where(ahead < 5, ahead, 2)
+    slabs_early = [(z - 2 + k + jnp.where(k >= skipped, 1, 0) + RING) % RING for k in range(4)]
+    slabs_late = [(z + offset) % RING for offset in (3, 5, 4)]
+    slabs_late = [jnp.where(slab == far_y, z, slab) for slab in slabs_late]
 
     def ladder(slabs):
         total = None
@@ -126,17 +130,7 @@
             total = product if total is None else total + product
         return total
 
-    def early_ladder():
-        slabs = []
-        for k in range(RING - 2):
-            slab = k + jnp.where(k >= low, 1, 0)
-            slabs.append(slab + jnp.where(slab >= high, 1, 0))
-        out_ref[...] = ladder(slabs)
-
-    def late_ladder():
-        out_ref[...] += ladder((far_y, far_z))
-
-    def core0():
+    def amplitudes(first_plane):
         friends = (*z_hop.values(), x_far, x_near)
         enter((sibling, *friends))
 
@@ -144,112 +138,147 @@
             products(part_0, *offsets)
             if offsets == (4,):
                 pl.semaphore_wait(go_sem, 1)
+                for _, piece in rotation(LONG):
+                    ref = part_0.at[piece_rows(4, piece)]
+                    send(1, ("p", 4, piece), ref, ref, sibling, 0)
+                return
             for offset in offsets:
                 ref = part_0.at[chunk_rows(offset)]
                 send(1, ("p", offsets[0]), ref, ref, sibling, 0)
 
-        load_a.wait()
-        reorder(0)
-        load_b.wait()
-        hand_products(4)
-        for k in (1, 3, 2):
-            reorder(k)
-        hand_products(3, -3)
-
-        def rows_x(pair, side):
-            return pl.ds(pl.multiple_of(pair * 128 + side * 64, 64), 64)
-
-        def rows_of(piece):
-            return rows_x(piece // 2, lo if piece % 2 else 1 - lo)
-
         def own(offset):
             return ((z + offset + RING) % RING) * 2 + hi
 
         def other(offset):
             return ((z + offset + RING) % RING) * 2 + 1 - hi
 
+        def half_rows(half):
+            return pl.ds(half * 128, 128)
+
+        def piece_of(slab, piece):
+            return t_all.at[piece % 2, slab, half_rows(piece // 2)]
+
         def z_send(s, distance, piece):
-            ref = t_all.at[:, own(-s * (distance - 1)), rows_of(piece)]
+            ref = piece_of(own(-s * (distance - 1)), piece)
             send(0, ("z", s, distance, piece), ref, ref, z_hop[s], 2)
 
         def far_send(offset, piece):
-            name = ("far", offset, piece if offset == 4 else piece // 2)
-            ref = t_all.at[:, own(offset), rows_of(piece)]
-            send(0, name, ref, ref, x_far, 3)
+            ref = piece_of(own(offset), piece)
+
+            def go():
+                send(0, ("far", offset, piece // 2), ref, ref, x_far, 3)
+
+            if offset != 4:
+                pl.when(lo == 1 - piece % 2)(go)
+            elif piece % 2:
+                send(1, "t last", ref, ref, x_far_sibling, 3)
+            else:
+                go()
 
         def z_arrived(s, distance, piece):
-            slab, rows = own(-s * distance), rows_of(piece)
-            arrived(0, ("z", s, distance, piece), t_all.at[:, slab, rows])
+            ref = piece_of(own(-s * distance), piece)
+            arrived(0, ("z", s, distance, piece), ref)
             if distance < (4 if piece in LONG[s] else 3):
                 z_send(s, distance + 1, piece)
-            if distance == 4:
-                far_send(4, piece)
-            elif piece % 2 == 0:
-                far_send(-s * distance, piece)
-            send(1, "t", t_all.at[1, slab, rows], t_all.at[1, slab, rows], sibling, 5)
-
-        def near(offset, pair):
-            slab, rows = other(offset), rows_x(pair, lo)
-            arrived(0, ("far", offset, pair), t_all.at[:, slab, rows])
-            ref0, ref1 = t_all.at[0, slab, rows], t_all.at[1, slab, rows]
-            send(0, "near", ref0, ref0, x_near, 4)
-            send(1, "t", ref1, ref1, x_near_sibling, 4)
-            send(1, "t", ref1, ref1, sibling, 6)
-
-        pl.semaphore_wait(barrier, len(friends))
-        pl.semaphore_signal(ready_sem, inc=1, device_id=x_near, device_id_type=MESH)
-        load_t.wait()
-        arrived(0, "t", t_all.at[1, ab])
-        for s, piece in rotation(LONG):
-            z_send(s, 1, piece)
-        for pair in range(2):
-            far_send(0, 2 * pair)
-        for s, piece in rotation(SHORT):
-            z_send(s, 1, piece)
-        hand_products(2, -2)
+            far_send(4 if distance == 4 else -s * distance, piece)
+            if piece % 2:
+                send(1, "t" if distance < 3 else "t last", ref, ref, sibling, 5)
+
+        def near(offset, half):
+            ref = t_all.at[lo, other(offset), half_rows(half)]
+            arrived(0, ("far", offset, half), ref)
+            late = " last" if abs(offset) == 3 else ""
+
+            def column_0():
+                send(0, "near" + late, ref, ref, x_near, 4)
+
+            def column_1():
+                send(1, "t" + late, ref, ref, x_near_sibling, 4)
+                send(1, "t" + late, ref, ref, sibling, 6)
+
+            pl.when(lo == 0)(column_0)
+            pl.when(lo == 1)(column_1)
+
+        def start_products():
+            load_a.wait()
+            reorder(0)
+            load_b.wait()
+            hand_products(4)
+            for k in (1, 3, 2):
+                reorder(k)
+
+        def start_column(col):
+            for pieces in (LONG, SHORT):
+                for s in (1, -1):
+                    z_send(s, 1, pieces[s][col])
+            for half in range(2):
+                far_send(0, 2 * half + col)
+
+        def start_amplitudes():
+            pl.semaphore_wait(barrier, len(friends))
+            load_t.wait()
+            start_column(0)
+
+        def second_column():
+            arrived(0, "t", t_all.at[1, ab])
+            start_column(1)
+            for friend in (x_near, x_far):
+                pl.semaphore_signal(ready_sem, inc=1, device_id=friend, device_id_type=MESH)
+
+        if first_plane:
+            start_products()
+            hand_products(3, -3)
+            hand_products(2, -2)
+            start_amplitudes()
+            second_column()
+        else:
+            start_amplitudes()
+            start_products()
+            second_column()
+            hand_products(3, -3)
+            hand_products(2, -2)
         hand_products(1, -1)
         hand_products(0)
         divisor()
+
         for distance in (1, 2, 3, 4):
             for pieces in (LONG, SHORT) if distance < 4 else (LONG,):
                 for s, piece in rotation(pieces):
                     z_arrived(s, distance, piece)
+                if distance > 1:
+                    for s in (1, -1):
+                        near(-s * (distance - 1), pieces[s][0] // 2)
             if distance == 1:
-                pl.semaphore_wait(ready_sem, 1)
-                for pair in range(2):
-                    near(0, pair)
-            else:
-                for s, pair in ((1, 0), (-1, 1), (1, 1), (-1, 0)):
-                    near(-s * (distance - 1), pair)
-        slab = other(4)
-        for _, piece in rotation(LONG):
-            rows = rows_x(piece // 2, 1 - lo if piece % 2 else lo)
-            arrived(0, ("far", 4, piece), t_all.at[:, slab, rows])
-            send(1, "t last", t_all.at[1, slab, rows], t_all.at[1, slab, rows], sibling, 1)
-        arrived(0, "near", t_all.at[0, 0:7, 0:128])
-
+                pl.semaphore_wait(ready_sem, 2)
+                for half in range(2):
+                    near(0, half)
+        for s in (1, -1):
+            near(-s * 3, SHORT[s][0] // 2)
+        for half in range(2):
+            arrived(0, ("far", 4, half), t_all.at[0, other(4), half_rows(half)])
+        pl.when(lo == 1)(lambda: arrived(0, "near", t_all.at[0, 0:5]))
         arrived(0, "g early", gath.at[0:7])
-        early_ladder()
+        out_ref[...] = ladder(slabs_early)
+        pl.when(lo == 1)(lambda: arrived(0, "near last", t_all.at[0, 0:2]))
+        out_ref[...] += ladder(slabs_late)
         arrived(0, "g last", gath.at[0])
-        late_ladder()
+        out_ref[...] += ladder([far_y])
 
         sent(0, part_0)
-        sent(1, t_all.at[0, 0])
         sent(2, t_all.at[0, 0:14])
         sent(3, t_all.at[0, 0:9])
         sent(4, t_all.at[0, 0:7])
         sent(5, t_all.at[0, 0:7])
-        sent(6, t_all.at[0, 0:7, 0:128])
-
-    def core1(ways):
+        pl.when(lo == 1)(lambda: sent(6, t_all.at[0, 0:7]))
+
+    def integrals(ways):
         enter(y_next.values())
         pl.semaphore_wait(barrier, 3)
         pl.semaphore_signal(go_sem, inc=1, device_id=sibling, device_id_type=MESH)
         send(0, "t", t_hbm, t_all.at[1, ab], sibling, 0)
 
         def own_part(offset, piece):
-            chip = (y + offset + RING) % RING
-            rows = pl.ds(pl.multiple_of(chip * 128 + piece * 32, 32), 32)
+            rows = piece_rows(offset, piece)
             return part[rows, :] + part_0[rows, :].astype(F32)
 
         def received(s, stage, piece):
@@ -276,8 +305,9 @@
         products(part, 4)
         products(part, 3, -3)
         products(part, 2, -2)
-        arrived(1, ("p", 4), part_0.at[0:128])
-        rs_stage(0, LONG)
+        for s, piece in rotation(LONG, ways):
+            arrived(1, ("p", 4, piece), part_0.at[0:32])
+            rs_send(s, 0, piece)
         arrived(1, ("p", 3), part_0.at[0:256])
         rs_stage(0, SHORT)
         products(part, 1, -1)
@@ -327,21 +357,22 @@
                     g_arrived(s, stage, piece)
         divisor()
         load_t.wait()
+        arrived(1, "t", t_all.at[1, 0:9])
+        out_ref[...] = ladder(slabs_early)
         for s, piece in rotation(LONG, ways):
             g_arrived(s, 3, piece)
-        arrived(1, "t", t_all.at[1, 0:14])
-        early_ladder()
-        arrived(1, "t last", t_all.at[1, 0])
-        late_ladder()
+        arrived(1, "t last", t_all.at[1, 0:6])
+        out_ref[...] += ladder([*slabs_late, far_y])
 
         sent(0, t_all.at[1, 0])
         sent(1, rs_out)
         sent(2, gath.at[0:7])
         sent(3, gath)
 
-    pl.when((core == 1) & (y % 4 < 2))(lambda: core1((-1, 1)))
-    pl.when((core == 1) & (y % 4 >= 2))(lambda: core1((1, -1)))
-    pl.when(core == 0)(core0)
+    pl.when((core == 1) & (y % 4 < 2))(lambda: integrals((-1, 1)))
+    pl.when((core == 1) & (y % 4 >= 2))(lambda: integrals((1, -1)))
+    pl.when((core == 0) & (z == 0))(lambda: amplitudes(True))
+    pl.when((core == 0) & (z > 0))(lambda: amplitudes(False))
     assert max(map(len, numbers)) <= N_RECV
 
 

time: 38 us -> 36.4 us (0.958)
  Pallas kernels: 36.4 us -> 34.8 us
    pallas_call x1, Pallas kernels: 36.4 us -> 34.8 us  [shards(): pl.pallas_call(kernel, out_shape=(result, result), in_specs=[hbm] * 6, ou...]
where the time goes in v5:
time: 36.4 us; the launch traced here: 36.2 us
  Pallas kernels  34.8 us (96%)
  other arithmetic  0.79 us (2%)
  between operations  0.66 us (2%)
    pallas_call x1, Pallas kernels, shards(): pl.pallas_call(kernel, out_shape=(result, result), in_specs=[hbm] * 6, ou...  34.8 us
    div x1, other arithmetic, shards(): residual / divisor.reshape(12, 16, 256).transpose(1, 0, 2)  0.79 us

profile of v5, /device:TPU:1, one launch (start us, length us, event | category | flops | bytes accessed | tf_op | source)
XLA Modules:
  0.0 36.2 jit_solution(14476714106510279215)
XLA Ops:
  0.6 0.0 copy-start
  0.6 34.8 %shard_map.86 = (f32[192,256]{1,0:T(8,128)S(1)}, f32[192,256]{1,0:T(8,128)S(1)}) custom-call(bf16[16,64,256]{2,1,0:T(8,128)(2,1)} %a_hbm.1, bf16[768,256]{1,0:T(8,128)(2,1)} %bitcast.13, bf16[256,256]{1,0:T(8,128)(2,1)} %bitcast.14, f32[1,16]{1,0:T(1,128)} %bitcast.16, f32[1,12]{1,0:T(1,128)} %bitcast.17, f32[1,256]{1,0:T(1,128)} %bitcast.15), custom_call_target="tpu_custom_call" | custom-call | flops 1207959552 | bytes 2097152 | tf_op jit(solution)/shard_map/pallas_call | solution.py:383
  35.4 0.0 copy-done
  35.5 0.8 %fusion = (f32[16,12,256]{2,0,1:T(8,128)}, f32[16,12,256]{2,0,1:T(8,128)}) fusion(f32[16,12,256]{2,0,1:T(8,128)S(1)} %bitcast.12, f32[16,12,256]{2,0,1:T(8,128)S(1)} %copy-done, f32[16,12,256]{2,0,1:T(8,128)S(1)} %bitcast.11), kind=kLoop, calls=%fused_computation | loop fusion | flops 98304 | bytes 983040 | tf_op jit(solution)/shard_map/div | solution.py:421
Async XLA Ops:
  0.6 34.8 %copy-start = (f32[16,12,256]{2,0,1:T(8,128)S(1)}, f32[16,12,256]{2,0,1:T(8,128)}, u32[]{:S(2)}) copy-start(f32[16,12,256]{2,0,1:T(8,128)} %param.10) | copy-start | bytes 589828

commit v6 on v5

--- a/solution.py
+++ b/solution.py
@@ -8,6 +8,7 @@
 MESH = pl.DeviceIdType.MESH
 BF16, F32 = jnp.bfloat16, jnp.float32
 RING = 8
+T_HOPS = {1: 3, -1: 4}
 PIECES = 4
 LONG = {1: (0, 1), -1: (2, 3)}
 SHORT = {1: (2, 3), -1: (0, 1)}
@@ -119,7 +120,8 @@
     skipped = jnp.where(ahead < 5, ahead, 2)
     slabs_early = [(z - 2 + k + jnp.where(k >= skipped, 1, 0) + RING) % RING for k in range(4)]
     slabs_late = [(z + offset) % RING for offset in (3, 5, 4)]
-    slabs_late = [jnp.where(slab == far_y, z, slab) for slab in slabs_late]
+    slab_between = jnp.where(ahead < 5, far_y, z)
+    slabs_late_y = [jnp.where(slab == far_y, z, slab) for slab in slabs_late]
 
     def ladder(slabs):
         total = None
@@ -169,7 +171,7 @@
                 send(0, ("far", offset, piece // 2), ref, ref, x_far, 3)
 
             if offset != 4:
-                pl.when(lo == 1 - piece % 2)(go)
+                pl.when(lo == piece % 2)(go)
             elif piece % 2:
                 send(1, "t last", ref, ref, x_far_sibling, 3)
             else:
@@ -178,14 +180,14 @@
         def z_arrived(s, distance, piece):
             ref = piece_of(own(-s * distance), piece)
             arrived(0, ("z", s, distance, piece), ref)
-            if distance < (4 if piece in LONG[s] else 3):
+            if distance < T_HOPS[s]:
                 z_send(s, distance + 1, piece)
             far_send(4 if distance == 4 else -s * distance, piece)
             if piece % 2:
                 send(1, "t" if distance < 3 else "t last", ref, ref, sibling, 5)
 
         def near(offset, half):
-            ref = t_all.at[lo, other(offset), half_rows(half)]
+            ref = t_all.at[1 - lo, other(offset), half_rows(half)]
             arrived(0, ("far", offset, half), ref)
             late = " last" if abs(offset) == 3 else ""
 
@@ -196,8 +198,8 @@
                 send(1, "t" + late, ref, ref, x_near_sibling, 4)
                 send(1, "t" + late, ref, ref, sibling, 6)
 
-            pl.when(lo == 0)(column_0)
-            pl.when(lo == 1)(column_1)
+            pl.when(lo == 1)(column_0)
+            pl.when(lo == 0)(column_1)
 
         def start_products():
             load_a.wait()
@@ -208,9 +210,9 @@
                 reorder(k)
 
         def start_column(col):
-            for pieces in (LONG, SHORT):
+            for half in range(2):
                 for s in (1, -1):
-                    z_send(s, 1, pieces[s][col])
+                    z_send(s, 1, 2 * half + col)
             for half in range(2):
                 far_send(0, 2 * half + col)
 
@@ -242,25 +244,28 @@
         divisor()
 
         for distance in (1, 2, 3, 4):
-            for pieces in (LONG, SHORT) if distance < 4 else (LONG,):
-                for s, piece in rotation(pieces):
+            ways = (1, -1) if distance <= T_HOPS[1] else (-1,)
+            for piece in (0, 2, 1, 3):
+                if distance == 4 and piece == 3:
+                    for s in (1, -1):
+                        near(-s * 3, 0)
+                for s in ways:
                     z_arrived(s, distance, piece)
-                if distance > 1:
+            if distance > 1:
+                for half in range(2) if distance < 4 else (1,):
                     for s in (1, -1):
-                        near(-s * (distance - 1), pieces[s][0] // 2)
+                        near(-s * (distance - 1), half)
             if distance == 1:
                 pl.semaphore_wait(ready_sem, 2)
                 for half in range(2):
                     near(0, half)
-        for s in (1, -1):
-            near(-s * 3, SHORT[s][0] // 2)
         for half in range(2):
             arrived(0, ("far", 4, half), t_all.at[0, other(4), half_rows(half)])
-        pl.when(lo == 1)(lambda: arrived(0, "near", t_all.at[0, 0:5]))
+        pl.when(lo == 0)(lambda: arrived(0, "near", t_all.at[0, 0:5]))
         arrived(0, "g early", gath.at[0:7])
         out_ref[...] = ladder(slabs_early)
-        pl.when(lo == 1)(lambda: arrived(0, "near last", t_all.at[0, 0:2]))
-        out_ref[...] += ladder(slabs_late)
+        pl.when(lo == 0)(lambda: arrived(0, "near last", t_all.at[0, 0:2]))
+        out_ref[...] += ladder(slabs_late_y)
         arrived(0, "g last", gath.at[0])
         out_ref[...] += ladder([far_y])
 
@@ -269,7 +274,7 @@
         sent(3, t_all.at[0, 0:9])
         sent(4, t_all.at[0, 0:7])
         sent(5, t_all.at[0, 0:7])
-        pl.when(lo == 1)(lambda: sent(6, t_all.at[0, 0:7]))
+        pl.when(lo == 0)(lambda: sent(6, t_all.at[0, 0:7]))
 
     def integrals(ways):
         enter(y_next.values())
@@ -361,8 +366,9 @@
         out_ref[...] = ladder(slabs_early)
         for s, piece in rotation(LONG, ways):
             g_arrived(s, 3, piece)
+        out_ref[...] += ladder([slab_between])
         arrived(1, "t last", t_all.at[1, 0:6])
-        out_ref[...] += ladder([*slabs_late, far_y])
+        out_ref[...] += ladder(slabs_late)
 
         sent(0, t_all.at[1, 0])
         sent(1, rs_out)

time: 36.4 us -> 35.9 us (0.986)
  Pallas kernels: 34.8 us -> 34.3 us
    pallas_call x1, Pallas kernels: 34.8 us -> 34.3 us  [shards(): pl.pallas_call(kernel, out_shape=(result, result), in_specs=[hbm] * 6, ou...]
where the time goes in v6:
time: 35.9 us; the launch traced here: 35.8 us
  Pallas kernels  34.3 us (96%)
  other arithmetic  0.79 us (2%)
  between operations  0.66 us (2%)
    pallas_call x1, Pallas kernels, shards(): pl.pallas_call(kernel, out_shape=(result, result), in_specs=[hbm] * 6, ou...  34.3 us
    div x1, other arithmetic, shards(): residual / divisor.reshape(12, 16, 256).transpose(1, 0, 2)  0.79 us

profile of v6, /device:TPU:1, one launch (start us, length us, event | category | flops | bytes accessed | tf_op | source)
XLA Modules:
  0.0 35.8 jit_solution(11700764610606843265)
XLA Ops:
  0.6 0.0 copy-start
  0.6 34.3 %shard_map.86 = (f32[192,256]{1,0:T(8,128)S(1)}, f32[192,256]{1,0:T(8,128)S(1)}) custom-call(bf16[16,64,256]{2,1,0:T(8,128)(2,1)} %a_hbm.1, bf16[768,256]{1,0:T(8,128)(2,1)} %bitcast.13, bf16[256,256]{1,0:T(8,128)(2,1)} %bitcast.14, f32[1,16]{1,0:T(1,128)} %bitcast.16, f32[1,12]{1,0:T(1,128)} %bitcast.17, f32[1,256]{1,0:T(1,128)} %bitcast.15), custom_call_target="tpu_custom_call" | custom-call | flops 1207959552 | bytes 2097152 | tf_op jit(solution)/shard_map/pallas_call | solution.py:389
  35.0 0.0 copy-done
  35.0 0.8 %fusion = (f32[16,12,256]{2,0,1:T(8,128)}, f32[16,12,256]{2,0,1:T(8,128)}) fusion(f32[16,12,256]{2,0,1:T(8,128)S(1)} %bitcast.12, f32[16,12,256]{2,0,1:T(8,128)S(1)} %copy-done, f32[16,12,256]{2,0,1:T(8,128)S(1)} %bitcast.11), kind=kLoop, calls=%fused_computation | loop fusion | flops 98304 | bytes 983040 | tf_op jit(solution)/shard_map/div | solution.py:427
Async XLA Ops:
  0.6 34.4 %copy-start = (f32[16,12,256]{2,0,1:T(8,128)S(1)}, f32[16,12,256]{2,0,1:T(8,128)}, u32[]{:S(2)}) copy-start(f32[16,12,256]{2,0,1:T(8,128)} %param.10) | copy-start | bytes 589828

commit v7 on v6

--- a/solution.py
+++ b/solution.py
@@ -85,15 +85,16 @@
         for load in (load_a, load_b, load_t, *loads_small):
             load.start()
 
-    row = lax.broadcasted_iota(jnp.int32, (256, 256), 0)
-    column = lax.broadcasted_iota(jnp.int32, (256, 256), 1)
-    swap = jnp.where(column == (row % 16) * 16 + row // 16, 1.0, 0.0).astype(BF16)
-
-    def reorder(k):
+    def swap():
+        row = lax.broadcasted_iota(jnp.int32, (256, 256), 0)
+        column = lax.broadcasted_iota(jnp.int32, (256, 256), 1)
+        return jnp.where(column == (row % 16) * 16 + row // 16, 1.0, 0.0).astype(BF16)
+
+    def reorder(k, matrix):
         block = ((y + 4) // 2 + k) % 4
         rows = a_in[:, pl.ds(pl.multiple_of(block * 16, 16), 16), :].reshape(256, 256)
         place = pl.ds(pl.multiple_of(block * 256, 256), 256)
-        a_all[place, :] = dot(swap, rows, ((1,), (0,))).astype(BF16)
+        a_all[place, :] = dot(matrix, rows, ((1,), (0,))).astype(BF16)
 
     def chunk_rows(offset):
         return pl.ds(pl.multiple_of(((y + offset + RING) % RING) * 128, 128), 128)
@@ -202,12 +203,13 @@
             pl.when(lo == 0)(column_1)
 
         def start_products():
+            matrix = swap()
             load_a.wait()
-            reorder(0)
+            reorder(0, matrix)
             load_b.wait()
             hand_products(4)
             for k in (1, 3, 2):
-                reorder(k)
+                reorder(k, matrix)
 
         def start_column(col):
             for half in range(2):
@@ -243,22 +245,31 @@
         hand_products(0)
         divisor()
 
-        for distance in (1, 2, 3, 4):
-            ways = (1, -1) if distance <= T_HOPS[1] else (-1,)
-            for piece in (0, 2, 1, 3):
-                if distance == 4 and piece == 3:
-                    for s in (1, -1):
-                        near(-s * 3, 0)
-                for s in ways:
+        turns = (0, 2, 1, 3)
+
+        def both(distance):
+            for piece in turns:
+                for s in (1, -1):
                     z_arrived(s, distance, piece)
-            if distance > 1:
-                for half in range(2) if distance < 4 else (1,):
-                    for s in (1, -1):
-                        near(-s * (distance - 1), half)
-            if distance == 1:
-                pl.semaphore_wait(ready_sem, 2)
-                for half in range(2):
-                    near(0, half)
+
+        def near_both(distance, half):
+            for s in (1, -1):
+                near(-s * distance, half)
+
+        both(1)
+        pl.semaphore_wait(ready_sem, 2)
+        for half in range(2):
+            near(0, half)
+        for distance in (2, 3):
+            both(distance)
+            for half in range(2):
+                near_both(distance - 1, half)
+        for piece in (0, 1):
+            z_arrived(-1, 4, piece)
+        near_both(3, 0)
+        for piece in (3, 2):
+            z_arrived(-1, 4, piece)
+        near_both(3, 1)
         for half in range(2):
             arrived(0, ("far", 4, half), t_all.at[0, other(4), half_rows(half)])
         pl.when(lo == 0)(lambda: arrived(0, "near", t_all.at[0, 0:5]))
@@ -303,9 +314,10 @@
             for s, piece in rotation(pieces, ways):
                 rs_send(s, stage, piece)
 
+        matrix = swap()
         load_a.wait()
         for k in range(4):
-            reorder(k)
+            reorder(k, matrix)
         load_b.wait()
         products(part, 4)
         products(part, 3, -3)

time: 35.9 us -> 35.2 us (0.981)
  Pallas kernels: 34.3 us -> 33.6 us
    pallas_call x1, Pallas kernels: 34.3 us -> 33.6 us  [shards(): pl.pallas_call(kernel, out_shape=(result, result), in_specs=[hbm] * 6, ou...]
where the time goes in v7:
time: 35.2 us; the launch traced here: 35.1 us
  Pallas kernels  33.6 us (95%)
  other arithmetic  0.79 us (2%)
  between operations  0.66 us (2%)
    pallas_call x1, Pallas kernels, shards(): pl.pallas_call(kernel, out_shape=(result, result), in_specs=[hbm] * 6, ou...  33.6 us
    div x1, other arithmetic, shards(): residual / divisor.reshape(12, 16, 256).transpose(1, 0, 2)  0.79 us

profile of v7, /device:TPU:1, one launch (start us, length us, event | category | flops | bytes accessed | tf_op | source)
XLA Modules:
  0.0 35.1 jit_solution(13795288112333060857)
XLA Ops:
  0.6 0.0 copy-start
  0.6 33.6 %shard_map.86 = (f32[192,256]{1,0:T(8,128)S(1)}, f32[192,256]{1,0:T(8,128)S(1)}) custom-call(bf16[16,64,256]{2,1,0:T(8,128)(2,1)} %a_hbm.1, bf16[768,256]{1,0:T(8,128)(2,1)} %bitcast.13, bf16[256,256]{1,0:T(8,128)(2,1)} %bitcast.14, f32[1,16]{1,0:T(1,128)} %bitcast.16, f32[1,12]{1,0:T(1,128)} %bitcast.17, f32[1,256]{1,0:T(1,128)} %bitcast.15), custom_call_target="tpu_custom_call" | custom-call | flops 1207959552 | bytes 2097152 | tf_op jit(solution)/shard_map/pallas_call | solution.py:401
  34.3 0.0 copy-done
  34.3 0.8 %fusion = (f32[16,12,256]{2,0,1:T(8,128)}, f32[16,12,256]{2,0,1:T(8,128)}) fusion(f32[16,12,256]{2,0,1:T(8,128)S(1)} %bitcast.12, f32[16,12,256]{2,0,1:T(8,128)S(1)} %copy-done, f32[16,12,256]{2,0,1:T(8,128)S(1)} %bitcast.11), kind=kLoop, calls=%fused_computation | loop fusion | flops 98304 | bytes 983040 | tf_op jit(solution)/shard_map/div | solution.py:439
Async XLA Ops:
  0.6 33.7 %copy-start = (f32[16,12,256]{2,0,1:T(8,128)S(1)}, f32[16,12,256]{2,0,1:T(8,128)}, u32[]{:S(2)}) copy-start(f32[16,12,256]{2,0,1:T(8,128)} %param.10) | copy-start | bytes 589828

commit v8 on v7

--- a/solution.py
+++ b/solution.py
@@ -122,7 +122,11 @@
     slabs_early = [(z - 2 + k + jnp.where(k >= skipped, 1, 0) + RING) % RING for k in range(4)]
     slabs_late = [(z + offset) % RING for offset in (3, 5, 4)]
     slab_between = jnp.where(ahead < 5, far_y, z)
-    slabs_late_y = [jnp.where(slab == far_y, z, slab) for slab in slabs_late]
+
+    def ladder_of(slabs, half):
+        left = [gath[slab, 2 * half + p] for slab in slabs for p in range(PIECES // 2)]
+        right = [t_all[core, 2 * slab + half] for slab in slabs]
+        return dot(jnp.concatenate(left, axis=1), jnp.concatenate(right, axis=0), ((1,), (0,)))
 
     def ladder(slabs):
         total = None
@@ -185,7 +189,7 @@
                 z_send(s, distance + 1, piece)
             far_send(4 if distance == 4 else -s * distance, piece)
             if piece % 2:
-                send(1, "t" if distance < 3 else "t last", ref, ref, sibling, 5)
+                send(1, "t" if distance < 3 else "t own", ref, ref, sibling, 5)
 
         def near(offset, half):
             ref = t_all.at[1 - lo, other(offset), half_rows(half)]
@@ -202,14 +206,11 @@
             pl.when(lo == 1)(column_0)
             pl.when(lo == 0)(column_1)
 
-        def start_products():
-            matrix = swap()
-            load_a.wait()
-            reorder(0, matrix)
-            load_b.wait()
-            hand_products(4)
+        def more_products():
             for k in (1, 3, 2):
                 reorder(k, matrix)
+            hand_products(3, -3)
+            hand_products(2, -2)
 
         def start_column(col):
             for half in range(2):
@@ -229,18 +230,19 @@
             for friend in (x_near, x_far):
                 pl.semaphore_signal(ready_sem, inc=1, device_id=friend, device_id_type=MESH)
 
+        matrix = swap()
+        if not first_plane:
+            start_amplitudes()
+        load_a.wait()
+        reorder(0, matrix)
+        load_b.wait()
+        hand_products(4)
         if first_plane:
-            start_products()
-            hand_products(3, -3)
-            hand_products(2, -2)
+            more_products()
             start_amplitudes()
-            second_column()
-        else:
-            start_amplitudes()
-            start_products()
-            second_column()
-            hand_products(3, -3)
-            hand_products(2, -2)
+        second_column()
+        if not first_plane:
+            more_products()
         hand_products(1, -1)
         hand_products(0)
         divisor()
@@ -270,15 +272,15 @@
         for piece in (3, 2):
             z_arrived(-1, 4, piece)
         near_both(3, 1)
-        for half in range(2):
-            arrived(0, ("far", 4, half), t_all.at[0, other(4), half_rows(half)])
         pl.when(lo == 0)(lambda: arrived(0, "near", t_all.at[0, 0:5]))
         arrived(0, "g early", gath.at[0:7])
         out_ref[...] = ladder(slabs_early)
+        arrived(0, "g last", gath.at[0])
+        out_ref[...] += ladder([slab_between]) + ladder_of(slabs_late, hi)
+        for half in range(2):
+            arrived(0, ("far", 4, half), t_all.at[0, other(4), half_rows(half)])
         pl.when(lo == 0)(lambda: arrived(0, "near last", t_all.at[0, 0:2]))
-        out_ref[...] += ladder(slabs_late_y)
-        arrived(0, "g last", gath.at[0])
-        out_ref[...] += ladder([far_y])
+        out_ref[...] += ladder_of(slabs_late, 1 - hi)
 
         sent(0, part_0)
         sent(2, t_all.at[0, 0:14])
@@ -378,9 +380,10 @@
         out_ref[...] = ladder(slabs_early)
         for s, piece in rotation(LONG, ways):
             g_arrived(s, 3, piece)
-        out_ref[...] += ladder([slab_between])
-        arrived(1, "t last", t_all.at[1, 0:6])
-        out_ref[...] += ladder(slabs_late)
+        arrived(1, "t own", t_all.at[1, 0:3])
+        out_ref[...] += ladder([slab_between]) + ladder_of(slabs_late, hi)
+        arrived(1, "t last", t_all.at[1, 0:3])
+        out_ref[...] += ladder_of(slabs_late, 1 - hi)
 
         sent(0, t_all.at[1, 0])
         sent(1, rs_out)

time: 35.2 us -> 35.1 us (level)
  no operation moved by 1% of the time
where the time goes in v8:
time: 35.1 us; the launch traced here: 34.9 us
  Pallas kernels  33.5 us (95%)
  other arithmetic  0.79 us (2%)
  between operations  0.66 us (2%)
    pallas_call x1, Pallas kernels, shards(): pl.pallas_call(kernel, out_shape=(result, result), in_specs=[hbm] * 6, ou...  33.5 us
    div x1, other arithmetic, shards(): residual / divisor.reshape(12, 16, 256).transpose(1, 0, 2)  0.79 us

profile of v8, /device:TPU:1, one launch (start us, length us, event | category | flops | bytes accessed | tf_op | source)
XLA Modules:
  0.0 34.9 jit_solution(1332411566875676962)
XLA Ops:
  0.6 0.0 copy-start
  0.6 33.5 %shard_map.86 = (f32[192,256]{1,0:T(8,128)S(1)}, f32[192,256]{1,0:T(8,128)S(1)}) custom-call(bf16[16,64,256]{2,1,0:T(8,128)(2,1)} %a_hbm.1, bf16[768,256]{1,0:T(8,128)(2,1)} %bitcast.13, bf16[256,256]{1,0:T(8,128)(2,1)} %bitcast.14, f32[1,16]{1,0:T(1,128)} %bitcast.16, f32[1,12]{1,0:T(1,128)} %bitcast.17, f32[1,256]{1,0:T(1,128)} %bitcast.15), custom_call_target="tpu_custom_call" | custom-call | flops 1207959552 | bytes 2097152 | tf_op jit(solution)/shard_map/pallas_call | solution.py:404
  34.1 0.0 copy-done
  34.2 0.8 %fusion = (f32[16,12,256]{2,0,1:T(8,128)}, f32[16,12,256]{2,0,1:T(8,128)}) fusion(f32[16,12,256]{2,0,1:T(8,128)S(1)} %bitcast.12, f32[16,12,256]{2,0,1:T(8,128)S(1)} %copy-done, f32[16,12,256]{2,0,1:T(8,128)S(1)} %bitcast.11), kind=kLoop, calls=%fused_computation | loop fusion | flops 98304 | bytes 983040 | tf_op jit(solution)/shard_map/div | solution.py:442
Async XLA Ops:
  0.6 33.5 %copy-start = (f32[16,12,256]{2,0,1:T(8,128)S(1)}, f32[16,12,256]{2,0,1:T(8,128)}, u32[]{:S(2)}) copy-start(f32[16,12,256]{2,0,1:T(8,128)} %param.10) | copy-start | bytes 589828

commit v9 on v8

--- a/solution.py
+++ b/solution.py
@@ -12,7 +12,7 @@
 PIECES = 4
 LONG = {1: (0, 1), -1: (2, 3)}
 SHORT = {1: (2, 3), -1: (0, 1)}
-N_RECV, N_SEND = 49, 7
+N_RECV, N_SEND = 42, 7
 
 
 SLOTS = {
@@ -20,6 +20,11 @@
         (s, stage, piece) for s in (1, -1) for stage in range(4) for piece in LONG[s] + (SHORT[s] if stage < 3 else ())
     )
 }
+
+
+REUSED = {(0, ("z", -1, 4, piece)): ("z", -1, 1, piece) for piece in range(PIECES)}
+REUSED |= {(0, ("far", 4, half)): ("far", 0, half) for half in range(2)}
+REUSED |= {(0, "g early"): "t"}
 
 
 def dot(a, b, dims):
@@ -49,6 +54,7 @@
     def recv_of(to, name):
         if isinstance(name, tuple) and name[0] == "g":
             name = ("rs", *name[1:])
+        name = REUSED.get((to, name), name)
         return recv_sem.at[numbers[to].setdefault(name, len(numbers[to]))]
 
     def send(to, name, src, dst, device, group):

time: 35.1 us -> 35 us (level)
  no operation moved by 1% of the time
where the time goes in v9:
time: 35 us; the launch traced here: 34.9 us
  Pallas kernels  33.4 us (95%)
  other arithmetic  0.79 us (2%)
  between operations  0.66 us (2%)
    pallas_call x1, Pallas kernels, shards(): pl.pallas_call(kernel, out_shape=(result, result), in_specs=[hbm] * 6, ou...  33.4 us
    div x1, other arithmetic, shards(): residual / divisor.reshape(12, 16, 256).transpose(1, 0, 2)  0.79 us

profile of v9, /device:TPU:1, one launch (start us, length us, event | category | flops | bytes accessed | tf_op | source)
XLA Modules:
  0.0 34.9 jit_solution(9809214717363003312)
XLA Ops:
  0.6 0.0 copy-start
  0.6 33.4 %shard_map.86 = (f32[192,256]{1,0:T(8,128)S(1)}, f32[192,256]{1,0:T(8,128)S(1)}) custom-call(bf16[16,64,256]{2,1,0:T(8,128)(2,1)} %a_hbm.1, bf16[768,256]{1,0:T(8,128)(2,1)} %bitcast.13, bf16[256,256]{1,0:T(8,128)(2,1)} %bitcast.14, f32[1,16]{1,0:T(1,128)} %bitcast.16, f32[1,12]{1,0:T(1,128)} %bitcast.17, f32[1,256]{1,0:T(1,128)} %bitcast.15), custom_call_target="tpu_custom_call" | custom-call | flops 1207959552 | bytes 2097152 | tf_op jit(solution)/shard_map/pallas_call | solution.py:410
  34.1 0.0 copy-done
  34.1 0.8 %fusion = (f32[16,12,256]{2,0,1:T(8,128)}, f32[16,12,256]{2,0,1:T(8,128)}) fusion(f32[16,12,256]{2,0,1:T(8,128)S(1)} %bitcast.12, f32[16,12,256]{2,0,1:T(8,128)S(1)} %copy-done, f32[16,12,256]{2,0,1:T(8,128)S(1)} %bitcast.11), kind=kLoop, calls=%fused_computation | loop fusion | flops 98304 | bytes 983040 | tf_op jit(solution)/shard_map/div | solution.py:448
Async XLA Ops:
  0.6 33.5 %copy-start = (f32[16,12,256]{2,0,1:T(8,128)S(1)}, f32[16,12,256]{2,0,1:T(8,128)}, u32[]{:S(2)}) copy-start(f32[16,12,256]{2,0,1:T(8,128)} %param.10) | copy-start | bytes 589828

commit v10 on v9

--- a/solution.py
+++ b/solution.py
@@ -88,7 +88,7 @@
     def enter(friends):
         for friend in friends:
             pl.semaphore_signal(barrier, inc=1, device_id=friend, device_id_type=MESH)
-        for load in (load_a, load_b, load_t, *loads_small):
+        for load in (load_t, load_a, load_b, *loads_small):
             load.start()
 
     def swap():
@@ -145,7 +145,7 @@
 
     def amplitudes(first_plane):
         friends = (*z_hop.values(), x_far, x_near)
-        enter((sibling, *friends))
+        enter((*friends, sibling))
 
         def hand_products(*offsets):
             products(part_0, *offsets)

time: 35 us -> 35 us (level)
  no operation moved by 1% of the time
where the time goes in v10:
time: 35 us; the launch traced here: 34.9 us
  Pallas kernels  33.4 us (95%)
  other arithmetic  0.79 us (2%)
  between operations  0.66 us (2%)
    pallas_call x1, Pallas kernels, shards(): pl.pallas_call(kernel, out_shape=(result, result), in_specs=[hbm] * 6, ou...  33.4 us
    div x1, other arithmetic, shards(): residual / divisor.reshape(12, 16, 256).transpose(1, 0, 2)  0.79 us

profile of v10, /device:TPU:1, one launch (start us, length us, event | category | flops | bytes accessed | tf_op | source)
XLA Modules:
  0.0 34.9 jit_solution(9651520014048330529)
XLA Ops:
  0.6 0.0 copy-start
  0.6 33.4 %shard_map.86 = (f32[192,256]{1,0:T(8,128)S(1)}, f32[192,256]{1,0:T(8,128)S(1)}) custom-call(bf16[16,64,256]{2,1,0:T(8,128)(2,1)} %a_hbm.1, bf16[768,256]{1,0:T(8,128)(2,1)} %bitcast.13, bf16[256,256]{1,0:T(8,128)(2,1)} %bitcast.14, f32[1,16]{1,0:T(1,128)} %bitcast.16, f32[1,12]{1,0:T(1,128)} %bitcast.17, f32[1,256]{1,0:T(1,128)} %bitcast.15), custom_call_target="tpu_custom_call" | custom-call | flops 1207959552 | bytes 2097152 | tf_op jit(solution)/shard_map/pallas_call | solution.py:410
  34.1 0.0 copy-done
  34.1 0.8 %fusion = (f32[16,12,256]{2,0,1:T(8,128)}, f32[16,12,256]{2,0,1:T(8,128)}) fusion(f32[16,12,256]{2,0,1:T(8,128)S(1)} %bitcast.12, f32[16,12,256]{2,0,1:T(8,128)S(1)} %copy-done, f32[16,12,256]{2,0,1:T(8,128)S(1)} %bitcast.11), kind=kLoop, calls=%fused_computation | loop fusion | flops 98304 | bytes 983040 | tf_op jit(solution)/shard_map/div | solution.py:448
Async XLA Ops:
  0.6 33.5 %copy-start = (f32[16,12,256]{2,0,1:T(8,128)S(1)}, f32[16,12,256]{2,0,1:T(8,128)}, u32[]{:S(2)}) copy-start(f32[16,12,256]{2,0,1:T(8,128)} %param.10) | copy-start | bytes 589828
